TPU v7x, 32 devices: a whole 2x2x4 slice. The times are simulated.
32 devices in a mesh: dp: 4 (over z), proto: 8 (over y, x, core).
Axes of the slice: x: 2, y: 2, z: 4, core: 2. Of those that a mesh axis runs over, the one named last changes fastest.
Arguments:
- embeddings: bfloat16 [8192, 2560], P('proto', 'dp'), may hold values from -26 to 26
- table: bfloat16 [32768, 2560], P('proto', 'dp'), may hold values from -5 to 5
- tile_lists: int32 [8, 8], replicated, may hold values from 0 to 255, as said below
- labels: int32 [8192], P('proto'), may hold values from 0 to 32767, as said below
Outputs:
- loss: float32 [], replicated
- grad_emb: bfloat16 [8192, 2560], P('proto', 'dp')
- grad_table: bfloat16 [32768, 2560], P('proto', 'dp')
Inputs may be any that keep to these rules, and one draw needn't show every extreme that they name: `tile_lists`: each block's 8 tile ids are distinct and fall on exactly 4 owners (owner = id // 32), each of those owners holding exactly 2 of them. `labels`: the tile of each row's label (label // 128) is in the list of the row's block.
All inputs are finite; a program needn't handle non-finite values.
Results may differ from a plain program's by a relative error of at most 0.0025.
The roundings to bfloat16 on the way count: a program that leaves them out, or rounds other values in their place, can miss the bound.
Values may be sent and summed in bfloat16 or wider, within the bound.
A program may use at most 128 MiB of HBM per device.

v0:
```python
import functools
import math

import jax
import jax.numpy as jnp
from jax import lax
from jax.experimental import pallas as pl
from jax.experimental.pallas import tpu as pltpu
from jax.sharding import PartitionSpec as P

D = 2560
TILE = 128
CAP = 2
CHUNK = 32
HALF = TILE // 2
LAG = 2
VMEM_LIMIT = 56 * 2**20
MESH = pl.DeviceIdType.MESH


def slot_plan(ids, tiles_here):
    owners = ids // tiles_here
    local = ids % tiles_here
    count = ids.shape[-1]
    before = jnp.arange(count)[:, None] > jnp.arange(count)[None, :]
    earlier = (owners[..., :, None] == owners[..., None, :]) & before
    rank = jnp.sum(earlier.astype(jnp.int32), axis=-1)
    return (owners, local, rank)


def softmax_terms(scores, ids, lab, list_len):
    hit = (ids[None, :] == (lab // TILE)[:, None]).astype(jnp.int32)
    column = (
        jnp.sum(hit * (jnp.arange(list_len, dtype=jnp.int32) * TILE)[None, :], axis=1) + lab % TILE
    )
    onehot = (jnp.arange(list_len * TILE, dtype=jnp.int32)[None, :] == column[:, None]).astype(
        jnp.float32
    )
    top = jnp.max(scores, axis=1, keepdims=True)
    expo = jnp.exp(scores - top)
    total = jnp.sum(expo, axis=1, keepdims=True)
    lse = top[:, 0] + jnp.log(total[:, 0])
    target = jnp.sum(scores * onehot, axis=1)
    dz_rows = (expo / total - onehot).astype(jnp.bfloat16)
    return (jnp.sum(lse - target), dz_rows)


def body(embeddings, table, tile_lists, labels):
    block_rows, width = embeddings.shape
    list_len = tile_lists.shape[1]
    tiles_here = table.shape[0] // TILE
    groups = lax.axis_size("proto")
    dp_count = lax.axis_size("dp")
    rows_dev = block_rows // dp_count
    total_rows = block_rows * groups
    me = lax.axis_index("proto")
    part = lax.axis_index("dp")
    inv_scale = 1.0 / math.sqrt(D)
    owners, local, rank = slot_plan(tile_lists, tiles_here)
    match = (owners == me)[:, :, None] & (
        rank[:, :, None] == jnp.arange(CAP, dtype=jnp.int32)[None, None, :]
    )
    select = jnp.sum(match.astype(jnp.int32) * local[:, :, None], axis=1)
    shaped_table = table.reshape(tiles_here, TILE, width)
    outgoing = pack_tiles(shaped_table, select.reshape(-1)).reshape(groups, CAP, TILE, width)
    incoming = lax.all_to_all(outgoing, "proto", split_axis=0, concat_axis=0, tiled=True)
    my_ids = lax.dynamic_index_in_dim(tile_lists, me, 0, keepdims=False)
    my_owner = lax.dynamic_index_in_dim(owners, me, 0, keepdims=False)
    my_rank = lax.dynamic_index_in_dim(rank, me, 0, keepdims=False)
    flat_slot = my_owner * CAP + my_rank
    tiles = pack_tiles(incoming.reshape(groups * CAP, TILE, width), flat_slot).reshape(
        list_len * TILE, width
    )
    scores = (
        lax.psum_scatter(
            lax.dot_general(
                embeddings, tiles, (((1,), (1,)), ((), ())), preferred_element_type=jnp.float32
            ),
            "dp",
            scatter_dimension=0,
            tiled=True,
        )
        * inv_scale
    )
    my_labels = lax.dynamic_slice_in_dim(labels, part * rows_dev, rows_dev, 0)
    loss_part, dz_rows = softmax_terms(scores, my_ids, my_labels, list_len)
    dz_block = lax.all_gather(dz_rows, "dp", axis=0, tiled=True)
    loss = lax.psum(loss_part, ("dp", "proto")) / total_rows
    grad_emb = jnp.dot(dz_block, tiles, preferred_element_type=jnp.float32).astype(jnp.bfloat16)
    piece = lax.dot_general(
        dz_block, embeddings, (((0,), (0,)), ((), ())), preferred_element_type=jnp.float32
    ).astype(jnp.bfloat16)
    returning = (
        jnp.zeros((groups * CAP, TILE, width), jnp.bfloat16)
        .at[flat_slot]
        .set(piece.reshape(list_len, TILE, width))
    )
    returned = lax.all_to_all(
        returning.reshape(groups, CAP, TILE, width),
        "proto",
        split_axis=0,
        concat_axis=0,
        tiled=True,
    )
    accum = (
        jnp.zeros((tiles_here, TILE, width), jnp.float32)
        .at[select.reshape(-1)]
        .add(returned.reshape(groups * CAP, TILE, width))
    )
    grad_table = accum.reshape(tiles_here * TILE, width).astype(jnp.bfloat16)
    return (loss, grad_emb, grad_table)


def pack_kernel(pick_ref, table_ref, out_ref, sems):
    count = out_ref.shape[0]

    def copy(slot):
        return pltpu.make_async_copy(
            table_ref.at[pick_ref[slot]], out_ref.at[slot], sems.at[slot]
        )

    for slot in range(count):
        copy(slot).start()
    for slot in range(count):
        copy(slot).wait()


def pack_tiles(shaped_table, pick):
    count = pick.shape[0]
    _, tile, width = shaped_table.shape
    return pl.pallas_call(
        pack_kernel,
        out_shape=jax.ShapeDtypeStruct((count, tile, width), shaped_table.dtype),
        grid_spec=pltpu.PrefetchScalarGridSpec(
            num_scalar_prefetch=1,
            grid=(1,),
            in_specs=[pl.BlockSpec(memory_space=pl.ANY)],
            out_specs=pl.BlockSpec(memory_space=pltpu.VMEM),
            scratch_shapes=[pltpu.SemaphoreType.DMA((count,))],
        ),
        compiler_params=pltpu.CompilerParams(vmem_limit_bytes=32 * 2**20),
    )(pick, shaped_table)


def place_kernel(per_step, count, pick_ref, uses_ref, first_ref, got_ref, emb_in, out_ref, emb_out, acc_ref):
    step = pl.program_id(0)
    emb_out[...] = emb_in[...]
    for inner in range(per_step):
        tile_id = step * per_step + inner
        uses = uses_ref[tile_id]

        @pl.when(uses == 0)
        def _():
            out_ref[inner] = jnp.zeros(out_ref.shape[1:], out_ref.dtype)

        @pl.when(uses == 1)
        def _():
            out_ref[inner] = got_ref[first_ref[tile_id]]

        @pl.when(uses > 1)
        def _():
            acc_ref[...] = jnp.zeros_like(acc_ref)

            def add(slot, carry):
                @pl.when(pick_ref[slot] == tile_id)
                def _():
                    acc_ref[...] += got_ref[slot].astype(jnp.float32)

                return carry

            lax.fori_loop(0, count, add, 0)
            out_ref[inner] = acc_ref[...].astype(out_ref.dtype)


def place_tiles(returned, pick, grad_emb, tiles_here):
    count, tile, width = returned.shape
    per_step = 4
    steps = tiles_here // per_step
    emb_spec = pl.BlockSpec((grad_emb.shape[0] // steps, width), lambda i, *refs: (i, 0))
    named = pick[None, :] == jnp.arange(tiles_here, dtype=jnp.int32)[:, None]
    uses = jnp.sum(named.astype(jnp.int32), axis=1)
    first = jnp.max(named * jnp.arange(count, dtype=jnp.int32)[None, :], axis=1)
    return pl.pallas_call(
        functools.partial(place_kernel, per_step, count),
        out_shape=(
            jax.ShapeDtypeStruct((tiles_here, tile, width), returned.dtype),
            jax.ShapeDtypeStruct(grad_emb.shape, grad_emb.dtype),
        ),
        grid_spec=pltpu.PrefetchScalarGridSpec(
            num_scalar_prefetch=3,
            grid=(steps,),
            in_specs=[pl.BlockSpec(memory_space=pltpu.VMEM), emb_spec],
            out_specs=(
                pl.BlockSpec((per_step, tile, width), lambda i, *refs: (i, 0, 0)),
                emb_spec,
            ),
            scratch_shapes=[pltpu.VMEM((tile, width), jnp.float32)],
        ),
        compiler_params=pltpu.CompilerParams(vmem_limit_bytes=24 * 2**20),
    )(pick, uses, first, returned, grad_emb)


def main_kernel(
    groups,
    dp_count,
    inv_scale,
    slot_ref,
    back_ref,
    out_tiles,
    emb,
    column,
    grad_emb,
    returned,
    loss_out,
    incoming_a,
    incoming_b,
    tiles,
    scores,
    partial,
    dz,
    piece,
    ret,
    loss_acc,
    loss_mine,
    loss_plane,
    loss_sum,
    loss_z,
    tile_send,
    tile_recv,
    own_sem,
    part_send,
    part_recv,
    dz_send,
    dz_recv,
    ret_send,
    ret_recv,
    own_ret_sem,
    lp_send,
    lp_recv,
    lz_send,
    lz_recv,
):
    me = lax.axis_index("proto")
    z = lax.axis_index("dp")
    rows, width = emb.shape
    list_len = slot_ref.shape[0]
    cols = list_len * TILE
    half = rows // 2
    chunks = half // CHUNK
    part_cols = cols // 2
    incoming = (incoming_a, incoming_b)
    last = dp_count - 1

    barrier = pltpu.get_barrier_semaphore()
    for k in range(1, groups):
        pl.semaphore_signal(
            barrier, inc=1, device_id={"proto": lax.rem(me + k, groups)}, device_id_type=MESH
        )
    for k in range(1, dp_count):
        pl.semaphore_signal(
            barrier, inc=1, device_id={"dp": lax.rem(z + k, dp_count)}, device_id_type=MESH
        )
    pl.semaphore_wait(barrier, groups + dp_count - 2)

    def tile_copy(h, k):
        to = lax.rem(me + k, groups)
        return pltpu.make_async_remote_copy(
            src_ref=out_tiles.at[pl.ds(to * CAP, CAP), pl.ds(h * HALF, HALF)],
            dst_ref=incoming[h].at[pl.ds(me * CAP, CAP)],
            send_sem=tile_send.at[h, k],
            recv_sem=tile_recv.at[h, k],
            device_id={"proto": to},
            device_id_type=MESH,
        )

    def own_copy(h):
        return pltpu.make_async_copy(
            out_tiles.at[pl.ds(me * CAP, CAP), pl.ds(h * HALF, HALF)],
            incoming[h].at[pl.ds(me * CAP, CAP)],
            own_sem.at[h],
        )

    def tiles_in(h):
        own_copy(h).wait()
        for k in range(1, groups):
            tile_copy(h, k).wait()
        for j in range(list_len):
            at = h * part_cols + j * HALF
            tiles[at : at + HALF, :] = incoming[h][slot_ref[j]]

    for h in range(2):
        for k in range(1, groups):
            tile_copy(h, k).start()
        own_copy(h).start()
    loss_acc[...] = jnp.zeros_like(loss_acc)
    tiles_in(0)

    block = min(256, half)
    group = 128 // CHUNK

    def rows_of(way, c):
        return pl.multiple_of((1 - way) * half + c * CHUNK, CHUNK)

    def part_copy(way, h, c, first):
        lanes = pl.ds(pl.multiple_of(h * part_cols, part_cols), part_cols)
        dst = partial.at[way, pl.ds(pl.multiple_of(c * CHUNK, CHUNK), CHUNK), lanes]
        src = scores.at[pl.ds(rows_of(way, c), CHUNK), lanes] if first else dst
        return pltpu.make_async_remote_copy(
            src_ref=src,
            dst_ref=dst,
            send_sem=part_send.at[way, h, c],
            recv_sem=part_recv.at[way, h, c],
            device_id={"dp": jnp.clip(z + 1 - 2 * way, 0, last)},
            device_id_type=MESH,
        )

    def dz_copy(way, c):
        at = dz.at[pl.ds(rows_of(way, c), CHUNK)]
        return pltpu.make_async_remote_copy(
            src_ref=at,
            dst_ref=at,
            send_sem=dz_send.at[way, c],
            recv_sem=dz_recv.at[way, c],
            device_id={"dp": jnp.clip(z - 1 + 2 * way, 0, last)},
            device_id_type=MESH,
        )

    lane = lax.broadcasted_iota(jnp.int32, (CHUNK, cols), 1)

    def step(i, carry):
        way = lax.rem(i, 2)
        s = i // 2
        pos = jnp.where(way == 0, z, last - z)
        turn = s - LAG * pos

        @pl.when((turn >= 0) & (turn < 2 * chunks))
        def _():
            h = turn // chunks
            c = lax.rem(turn, chunks)
            lanes = pl.ds(pl.multiple_of(h * part_cols, part_cols), part_cols)

            @pl.when(lax.rem(c, group) == 0)
            def _():
                these = pl.ds(rows_of(way, c), group * CHUNK)
                scores[these, lanes] = lax.dot_general(
                    emb[these, :],
                    tiles[lanes, :],
                    (((1,), (1,)), ((), ())),
                    preferred_element_type=jnp.float32,
                )

            at = pl.ds(rows_of(way, c), CHUNK)
            here = pl.ds(pl.multiple_of(c * CHUNK, CHUNK), CHUNK)

            @pl.when(pos == 0)
            def _():
                part_copy(way, h, c, True).start()

            @pl.when((pos > 0) & (pos < last))
            def _():
                part_copy(way, h, c, False).wait_recv()
                partial[way, here, lanes] += scores[at, lanes]
                part_copy(way, h, c, False).start()

            @pl.when((pos == last) & (h == 1))
            def _():
                part_copy(way, 0, c, False).wait_recv()
                part_copy(way, 1, c, False).wait_recv()
                score = (partial[way, here, :] + scores[at, :]) * inv_scale
                onehot = lane == column[at, :]
                top = jnp.max(score, axis=1, keepdims=True)
                expo = jnp.exp(score - top)
                total = jnp.sum(expo, axis=1, keepdims=True)
                target = jnp.sum(jnp.where(onehot, score, 0.0), axis=1, keepdims=True)
                loss_acc[...] += (top + jnp.log(total)) - target + jnp.zeros_like(loss_acc)
                dz[at, :] = (expo / total - jnp.where(onehot, 1.0, 0.0)).astype(dz.dtype)
                dz_copy(way, c).start()

        c2 = s - chunks - LAG * last - LAG * (last - pos)

        @pl.when((c2 >= 0) & (c2 < chunks) & (pos < last))
        def _():
            dz_copy(way, c2).wait_recv()

            @pl.when(pos > 0)
            def _():
                dz_copy(way, c2).start()

        return carry

    lax.fori_loop(0, 2 * chunks, step, 0)
    tiles_in(1)
    lax.fori_loop(2 * chunks, 2 * (2 * chunks + 2 * LAG * last), step, 0)

    loss_mine[...] = jnp.broadcast_to(jnp.sum(loss_acc[...], axis=0, keepdims=True), (8, 128))

    def lp_copy(k):
        return pltpu.make_async_remote_copy(
            src_ref=loss_mine,
            dst_ref=loss_plane.at[me],
            send_sem=lp_send.at[k],
            recv_sem=lp_recv.at[k],
            device_id={"proto": lax.rem(me + k, groups)},
            device_id_type=MESH,
        )

    for k in range(1, groups):
        lp_copy(k).start()

    wide = min(256, cols)
    for j in range(cols // wide):
        out = lax.dot_general(
            dz[:, j * wide : (j + 1) * wide],
            emb[...],
            (((0,), (0,)), ((), ())),
            preferred_element_type=jnp.float32,
        ).astype(piece.dtype)
        for t in range(wide // HALF):
            h, tile = divmod(j * (wide // HALF) + t, list_len)
            piece[tile, h * HALF : (h + 1) * HALF, :] = out[t * HALF : (t + 1) * HALF, :]

    def ret_copy(k):
        to = lax.rem(me + k, groups)
        return pltpu.make_async_remote_copy(
            src_ref=ret.at[pl.ds(to * CAP, CAP)],
            dst_ref=returned.at[pl.ds(me * CAP, CAP)],
            send_sem=ret_send.at[k],
            recv_sem=ret_recv.at[k],
            device_id={"proto": to},
            device_id_type=MESH,
        )

    for k in range(1, groups):
        to = lax.rem(me + k, groups)
        for t in range(CAP):
            ret[to * CAP + t] = piece[back_ref[to * CAP + t]]
        ret_copy(k).start()
    for t in range(CAP):
        ret[me * CAP + t] = piece[back_ref[me * CAP + t]]
    own_ret = pltpu.make_async_copy(
        ret.at[pl.ds(me * CAP, CAP)], returned.at[pl.ds(me * CAP, CAP)], own_ret_sem
    )
    own_ret.start()

    def grad_block(i, carry):
        at = pl.ds(pl.multiple_of(i * block, block), block)
        grad_emb[at, :] = jnp.dot(
            dz[at, :], tiles[...], preferred_element_type=jnp.float32
        ).astype(grad_emb.dtype)
        return carry

    lax.fori_loop(0, rows // block, grad_block, 0)

    loss_plane[me] = loss_mine[...]
    for k in range(1, groups):
        lp_copy(k).wait()
    plane = loss_plane[0]
    for k in range(1, groups):
        plane = plane + loss_plane[k]
    loss_sum[...] = plane

    def lz_copy(k):
        return pltpu.make_async_remote_copy(
            src_ref=loss_sum,
            dst_ref=loss_z.at[z],
            send_sem=lz_send.at[k],
            recv_sem=lz_recv.at[k],
            device_id={"dp": lax.rem(z + k, dp_count)},
            device_id_type=MESH,
        )

    for k in range(1, dp_count):
        lz_copy(k).start()
    loss_z[z] = plane
    for k in range(1, dp_count):
        lz_copy(k).wait()
    whole = loss_z[0]
    for k in range(1, dp_count):
        whole = whole + loss_z[k]
    loss_out[...] = whole

    def drain(i, carry):
        way = lax.rem(i, 2)
        c = i // 2
        pos = jnp.where(way == 0, z, last - z)

        @pl.when(pos < last)
        def _():
            part_copy(way, 0, c, False).wait_send()
            part_copy(way, 1, c, False).wait_send()

        @pl.when(pos > 0)
        def _():
            dz_copy(way, c).wait_send()

        return carry

    lax.fori_loop(0, 2 * chunks, drain, 0)
    own_ret.wait()
    for k in range(1, groups):
        ret_copy(k).wait()


def fused_body(embeddings, table, tile_lists, labels):
    block_rows, width = embeddings.shape
    list_len = tile_lists.shape[1]
    tiles_here = table.shape[0] // TILE
    groups = lax.axis_size("proto")
    dp_count = lax.axis_size("dp")
    total_rows = block_rows * groups
    cols = list_len * TILE
    slots = groups * CAP
    me = lax.axis_index("proto")
    owners, local, rank = slot_plan(tile_lists, tiles_here)
    match = (owners == me)[:, :, None] & (
        rank[:, :, None] == jnp.arange(CAP, dtype=jnp.int32)[None, None, :]
    )
    select = jnp.sum(match.astype(jnp.int32) * local[:, :, None], axis=1).reshape(-1)
    taken = jnp.any(match, axis=1).reshape(-1)
    my_ids = lax.dynamic_index_in_dim(tile_lists, me, 0, keepdims=False)
    flat = owners * CAP + rank
    my_slot = lax.dynamic_index_in_dim(flat, me, 0, keepdims=False)
    order = jnp.arange(list_len, dtype=jnp.int32)
    back = jnp.sum(
        (my_slot[None, :] == jnp.arange(slots, dtype=jnp.int32)[:, None]).astype(jnp.int32)
        * order[None, :],
        axis=1,
    )
    hit = (my_ids[None, :] == (labels // TILE)[:, None]).astype(jnp.int32)
    within = labels % TILE
    column = (
        jnp.sum(hit * (order * HALF)[None, :], axis=1)
        + within // HALF * (cols // 2)
        + within % HALF
    )[:, None]
    outgoing = pack_tiles(table.reshape(tiles_here, TILE, width), select)
    chunks = block_rows // 2 // CHUNK
    bf16, f32 = jnp.bfloat16, jnp.float32
    dma = pltpu.SemaphoreType.DMA
    vmem = pl.BlockSpec(memory_space=pltpu.VMEM)
    smem = pl.BlockSpec(memory_space=pltpu.SMEM)
    hbm = pl.BlockSpec(memory_space=pl.ANY)
    grad_emb, returned, loss = pl.pallas_call(
        functools.partial(main_kernel, groups, dp_count, 1.0 / math.sqrt(D)),
        out_shape=(
            jax.ShapeDtypeStruct((block_rows, width), bf16),
            jax.ShapeDtypeStruct((slots, TILE, width), bf16),
            jax.ShapeDtypeStruct((8, 128), f32),
        ),
        in_specs=[smem, smem, hbm, vmem, vmem],
        out_specs=(vmem, hbm, vmem),
        scratch_shapes=[
            pltpu.VMEM((slots, HALF, width), bf16),
            pltpu.VMEM((slots, HALF, width), bf16),
            pltpu.VMEM((cols, width), bf16),
            pltpu.VMEM((block_rows, cols), f32),
            pltpu.VMEM((2, block_rows // 2, cols), f32),
            pltpu.VMEM((block_rows, cols), bf16),
            pltpu.VMEM((list_len, TILE, width), bf16),
            pltpu.VMEM((slots, TILE, width), bf16),
            pltpu.VMEM((CHUNK, 128), f32),
            pltpu.VMEM((8, 128), f32),
            pltpu.VMEM((groups, 8, 128), f32),
            pltpu.VMEM((8, 128), f32),
            pltpu.VMEM((dp_count, 8, 128), f32),
            dma((2, groups)),
            dma((2, groups)),
            dma((2,)),
            dma((2, 2, chunks)),
            dma((2, 2, chunks)),
            dma((2, chunks)),
            dma((2, chunks)),
            dma((groups,)),
            dma((groups,)),
            dma,
            dma((groups,)),
            dma((groups,)),
            dma((dp_count,)),
            dma((dp_count,)),
        ],
        compiler_params=pltpu.CompilerParams(
            collective_id=0, has_side_effects=True, vmem_limit_bytes=VMEM_LIMIT
        ),
    )(my_slot, back, outgoing, embeddings, column)
    grad_table, grad_emb = place_tiles(
        returned, jnp.where(taken, select, -1), grad_emb, tiles_here
    )
    return (loss[0, 0] / total_rows, grad_emb, grad_table.reshape(tiles_here * TILE, width))


def fused_bytes(block_rows, width, list_len, groups):
    cols = list_len * TILE
    slots = groups * CAP
    return (
        block_rows * cols * (4 + 4 + 2)
        + 2 * slots * TILE * width * 2
        + 2 * cols * width * 2
        + 2 * block_rows * width * 2
        + block_rows * 128 * 4
    )


def any_body(embeddings, table, tile_lists, labels):
    need = fused_bytes(*embeddings.shape, tile_lists.shape[1], lax.axis_size("proto"))
    if need + 12 * 2**20 <= VMEM_LIMIT:
        return fused_body(embeddings, table, tile_lists, labels)
    return body(embeddings, table, tile_lists, labels)


def solution(mesh):
    placed = (P("proto", "dp"), P("proto", "dp"), P(), P("proto"))
    return jax.shard_map(
        any_body,
        mesh=mesh,
        in_specs=placed,
        out_specs=(P(), P("proto", "dp"), P("proto", "dp")),
        check_vma=False,
    )
```

profile of v0, /device:TPU:0, one launch (start us, length us, event | category | flops | bytes accessed | tf_op | source)
XLA Modules:
  0.0 163.4 jit_solution(12263038608385144567)
XLA Ops:
  0.6 0.7 dynamic-slice_bitcast_fusion
  1.3 0.7 add_select_fusion.3
  2.0 0.1 select_reduce_fusion
  2.1 0.7 fusion.4
  2.8 0.7 add_select_fusion.4
  3.5 0.7 broadcast_compare_fusion
  4.2 0.3 convert_reduce_fusion
  4.5 0.2 select_reduce_fusion.2
  4.7 0.2 fusion.1
  4.8 0.0 copy-start.4
  4.9 0.6 select_reduce_fusion.3.back_ref
  5.5 0.1 copy.10
  5.6 0.1 reshape.53
  5.7 0.1 copy.8
  5.7 0.1 reshape.51.pick_ref
  5.8 0.1 select_reduce_fusion.1
  5.9 1.0 copy.9.column
  7.0 0.0 copy-start.1
  7.0 2.5 %copy-done.1 = bf16[4096,640]{1,0:T(8,128)(2,1)S(1)} copy-done((bf16[4096,640]{1,0:T(8,128)(2,1)S(1)}, bf16[4096,640]{1,0:T(8,128)(2,1)}, u32[]{:S(2)}) %copy-start.1) | copy-done | bytes 5242904
  9.4 4.1 %shard_map.67.out_tiles = bf16[16,128,640]{2,1,0:T(8,128)(2,1)S(1)} custom-call(s32[16]{0:T(128)S(1)} %reshape.51.pick_ref, bf16[32,128,640]{2,1,0:T(8,128)(2,1)S(1)} %bitcast.8), custom_call_target="tpu_custom_call" | custom-call | tf_op jit(solution)/shard_map/pallas_call | solution.py:131
  13.6 0.0 copy-done.4
  13.6 0.0 copy-start
  13.6 1.5 copy-done
  15.1 137.5 %shard_map.68 = (bf16[1024,640]{1,0:T(8,128)(2,1)}, bf16[16,128,640]{2,1,0:T(8,128)(2,1)}, f32[8,128]{1,0:T(8,128)}) custom-call(s32[8]{0:T(128)} %copy-done.4, s32[16]{0:T(128)} %select_reduce_fusion.3.back_ref, bf16[16,128,640]{2,1,0:T(8,128)(2,1)} %copy-done, bf16[1024,640]{1,0:T(8,128)(2,1)} %emb.1, s32[1024,1]{1,0:T(8,128)} %copy.9.column), custom_call_target="tpu_custom_call" | custom-call | tf_op jit(solution)/shard_map/pallas_call | solution.py:543
  152.6 1.2 slice.3
  154.4 0.0 copy-start.2
  154.4 1.7 %copy-done.2 = bf16[16,128,640]{2,1,0:T(8,128)(2,1)S(1)} copy-done((bf16[16,128,640]{2,1,0:T(8,128)(2,1)S(1)}, bf16[16,128,640]{2,1,0:T(8,128)(2,1)}, u32[]{:S(2)}) %copy-start.2) | copy-done | bytes 2621464
  156.1 0.0 copy-start.3
  156.1 1.3 copy-done.3
  157.5 4.8 %shard_map.69 = (bf16[32,128,640]{2,1,0:T(8,128)(2,1)}, bf16[1024,640]{1,0:T(8,128)(2,1)}) custom-call(s32[16]{0:T(128)S(1)} %broadcast_select_fusion.pick_ref, s32[32]{0:T(128)S(1)} %get-tuple-element.14.uses_ref, s32[32]{0:T(128)S(1)} %get-tuple-element.13.first_ref, bf16[16,128,640]{2,1,0:T(8,128)(2,1)S(1)} %copy-done.2, bf16[1024,640]{1,0:T(8,128)(2,1)S(1)} %copy-done.3), custom_call_target="tpu_custom_call" | custom-call | tf_op jit(solution)/shard_map/pallas_call | solution.py:183
  (4 shorter events, 0.0 us)
Async XLA Ops:
  4.8 8.8 %copy-start.4 = (s32[8]{0:T(128)}, s32[8]{0:T(128)S(1)}, u32[]{:S(2)}) copy-start(s32[8]{0:T(128)S(1)} %dynamic-slice_bitcast_fusion.1.slot_ref) | copy-start | bytes 100
  7.0 2.5 %copy-start.1 = (bf16[4096,640]{1,0:T(8,128)(2,1)S(1)}, bf16[4096,640]{1,0:T(8,128)(2,1)}, u32[]{:S(2)}) copy-start(bf16[4096,640]{1,0:T(8,128)(2,1)} %param.5) | copy-start | bytes 15728644
  13.6 1.5 copy-start
  154.4 1.7 %copy-start.2 = (bf16[16,128,640]{2,1,0:T(8,128)(2,1)S(1)}, bf16[16,128,640]{2,1,0:T(8,128)(2,1)}, u32[]{:S(2)}) copy-start(bf16[16,128,640]{2,1,0:T(8,128)(2,1)} %get-tuple-element.9.got_ref) | copy-start | bytes 7864324
  156.1 1.3 copy-start.3
where the time goes:
time: 164 us; the launch traced here: 163 us
  Pallas kernels  146 us (89%)
  local copies, waits for them, and re-layouts  10.3 us (6%)
  other arithmetic  4.2 us (3%)
  between operations  2.5 us (2%)
    pallas_call x1, Pallas kernels, fused_body(): pl.pallas_call(functools.partial(main_kernel, groups, dp_count, 1.0 / mat...  137 us
    unnamed x10, local copies, waits for them, and re-layouts  7.03 us
    pallas_call x1, Pallas kernels, place_tiles(): pl.pallas_call(functools.partial(place_kernel, per_step, count), out_shap...  4.85 us
    pallas_call x1, Pallas kernels, pack_tiles(): pl.pallas_call(pack_kernel, out_shape=jax.ShapeDtypeStruct((count, tile,...  4.14 us

commit v1 on v0

v1 whole, which is shorter than its diff:
```python
import functools
import math

import jax
import jax.numpy as jnp
from jax import lax
from jax.experimental import pallas as pl
from jax.experimental.pallas import tpu as pltpu
from jax.sharding import PartitionSpec as P

D = 2560
TILE = 128
CAP = 2
PARTS = 4
CHUNK = {False: 32, True: 64}
DZ_CHUNK = 64
LAG = 4
DZ_LAG = 4
CODED = False
CODE_MAX = 32766.0
ROUND = 12582912.0
VMEM_LIMIT = 56 * 2**20
MESH = pl.DeviceIdType.MESH


def slot_plan(ids, tiles_here):
    owners = ids // tiles_here
    local = ids % tiles_here
    count = ids.shape[-1]
    before = jnp.arange(count)[:, None] > jnp.arange(count)[None, :]
    earlier = (owners[..., :, None] == owners[..., None, :]) & before
    rank = jnp.sum(earlier.astype(jnp.int32), axis=-1)
    return (owners, local, rank)


def softmax_terms(scores, ids, lab, list_len):
    hit = (ids[None, :] == (lab // TILE)[:, None]).astype(jnp.int32)
    column = (
        jnp.sum(hit * (jnp.arange(list_len, dtype=jnp.int32) * TILE)[None, :], axis=1) + lab % TILE
    )
    onehot = (jnp.arange(list_len * TILE, dtype=jnp.int32)[None, :] == column[:, None]).astype(
        jnp.float32
    )
    top = jnp.max(scores, axis=1, keepdims=True)
    expo = jnp.exp(scores - top)
    total = jnp.sum(expo, axis=1, keepdims=True)
    lse = top[:, 0] + jnp.log(total[:, 0])
    target = jnp.sum(scores * onehot, axis=1)
    dz_rows = (expo / total - onehot).astype(jnp.bfloat16)
    return (jnp.sum(lse - target), dz_rows)


def body(embeddings, table, tile_lists, labels):
    block_rows, width = embeddings.shape
    list_len = tile_lists.shape[1]
    tiles_here = table.shape[0] // TILE
    groups = lax.axis_size("proto")
    dp_count = lax.axis_size("dp")
    rows_dev = block_rows // dp_count
    total_rows = block_rows * groups
    me = lax.axis_index("proto")
    part = lax.axis_index("dp")
    inv_scale = 1.0 / math.sqrt(D)
    owners, local, rank = slot_plan(tile_lists, tiles_here)
    match = (owners == me)[:, :, None] & (
        rank[:, :, None] == jnp.arange(CAP, dtype=jnp.int32)[None, None, :]
    )
    select = jnp.sum(match.astype(jnp.int32) * local[:, :, None], axis=1)
    shaped_table = table.reshape(tiles_here, TILE, width)
    outgoing = pack_tiles(shaped_table, select.reshape(-1)).reshape(groups, CAP, TILE, width)
    incoming = lax.all_to_all(outgoing, "proto", split_axis=0, concat_axis=0, tiled=True)
    my_ids = lax.dynamic_index_in_dim(tile_lists, me, 0, keepdims=False)
    my_owner = lax.dynamic_index_in_dim(owners, me, 0, keepdims=False)
    my_rank = lax.dynamic_index_in_dim(rank, me, 0, keepdims=False)
    flat_slot = my_owner * CAP + my_rank
    tiles = pack_tiles(incoming.reshape(groups * CAP, TILE, width), flat_slot).reshape(
        list_len * TILE, width
    )
    scores = (
        lax.psum_scatter(
            lax.dot_general(
                embeddings, tiles, (((1,), (1,)), ((), ())), preferred_element_type=jnp.float32
            ),
            "dp",
            scatter_dimension=0,
            tiled=True,
        )
        * inv_scale
    )
    my_labels = lax.dynamic_slice_in_dim(labels, part * rows_dev, rows_dev, 0)
    loss_part, dz_rows = softmax_terms(scores, my_ids, my_labels, list_len)
    dz_block = lax.all_gather(dz_rows, "dp", axis=0, tiled=True)
    loss = lax.psum(loss_part, ("dp", "proto")) / total_rows
    grad_emb = jnp.dot(dz_block, tiles, preferred_element_type=jnp.float32).astype(jnp.bfloat16)
    piece = lax.dot_general(
        dz_block, embeddings, (((0,), (0,)), ((), ())), preferred_element_type=jnp.float32
    ).astype(jnp.bfloat16)
    returning = (
        jnp.zeros((groups * CAP, TILE, width), jnp.bfloat16)
        .at[flat_slot]
        .set(piece.reshape(list_len, TILE, width))
    )
    returned = lax.all_to_all(
        returning.reshape(groups, CAP, TILE, width),
        "proto",
        split_axis=0,
        concat_axis=0,
        tiled=True,
    )
    accum = (
        jnp.zeros((tiles_here, TILE, width), jnp.float32)
        .at[select.reshape(-1)]
        .add(returned.reshape(groups * CAP, TILE, width))
    )
    grad_table = accum.reshape(tiles_here * TILE, width).astype(jnp.bfloat16)
    return (loss, grad_emb, grad_table)


def pack_kernel(pick_ref, table_ref, out_ref, sems):
    count = out_ref.shape[0]

    def copy(slot):
        return pltpu.make_async_copy(
            table_ref.at[pick_ref[slot]], out_ref.at[slot], sems.at[slot]
        )

    for slot in range(count):
        copy(slot).start()
    for slot in range(count):
        copy(slot).wait()


def pack_tiles(shaped_table, pick):
    count = pick.shape[0]
    _, tile, width = shaped_table.shape
    return pl.pallas_call(
        pack_kernel,
        out_shape=jax.ShapeDtypeStruct((count, tile, width), shaped_table.dtype),
        grid_spec=pltpu.PrefetchScalarGridSpec(
            num_scalar_prefetch=1,
            grid=(1,),
            in_specs=[pl.BlockSpec(memory_space=pl.ANY)],
            out_specs=pl.BlockSpec(memory_space=pltpu.VMEM),
            scratch_shapes=[pltpu.SemaphoreType.DMA((count,))],
        ),
        compiler_params=pltpu.CompilerParams(vmem_limit_bytes=32 * 2**20),
    )(pick, shaped_table)


def place_kernel(lists, returned, emb_in, loss_in, table_out, emb_out, loss_out, got, emb, zero, sums, count, first, second, slots, in_sem, emb_sem, out_sem):
    me = lax.axis_index("proto")
    blocks, list_len = lists.shape
    tiles_here = table_out.shape[0]
    load = pltpu.make_async_copy(returned, got, in_sem)
    load.start()
    load_emb = pltpu.make_async_copy(emb_in, emb, emb_sem)
    load_emb.start()
    zero[...] = jnp.zeros_like(zero)
    base = me * tiles_here

    def clear(t, carry):
        count[t] = 0
        first[t] = 0
        return carry

    lax.fori_loop(0, tiles_here, clear, 0)

    def note(b, carry):
        slots[0] = b * CAP
        for j in range(list_len):
            tile = lists[b, j] - base

            @pl.when((tile >= 0) & (tile < tiles_here))
            def _():
                seen = count[tile]
                second[tile] = first[tile]
                first[tile] = slots[0]
                count[tile] = seen + 1
                slots[0] = slots[0] + 1

        return carry

    lax.fori_loop(0, blocks, note, 0)

    def from_zero(t):
        return pltpu.make_async_copy(zero, table_out.at[t], out_sem.at[t])

    def zeros(t, carry):
        @pl.when(count[t] == 0)
        def _():
            from_zero(t).start()

        return carry

    lax.fori_loop(0, tiles_here, zeros, 0)
    loss_out[0, 0] = jnp.max(loss_in[0:1, :])
    load_emb.wait()
    save_emb = pltpu.make_async_copy(emb, emb_out, emb_sem)
    save_emb.start()
    load.wait()

    def ones(t, carry):
        @pl.when(count[t] == 1)
        def _():
            pltpu.make_async_copy(got.at[first[t]], table_out.at[t], out_sem.at[t]).start()

        return carry

    lax.fori_loop(0, tiles_here, ones, 0)

    def many(t, carry):
        @pl.when(count[t] == 2)
        def _():
            total = got[first[t]].astype(jnp.float32) + got[second[t]].astype(jnp.float32)
            got[first[t]] = total.astype(got.dtype)
            pltpu.make_async_copy(got.at[first[t]], table_out.at[t], out_sem.at[t]).start()

        @pl.when(count[t] > 2)
        def _():
            sums[...] = jnp.zeros_like(sums)

            def block(b, carry):
                slots[0] = b * CAP
                for j in range(list_len):
                    tile = lists[b, j] - base

                    @pl.when((tile >= 0) & (tile < tiles_here))
                    def _():
                        @pl.when(tile == t)
                        def _():
                            sums[...] += got[slots[0]].astype(jnp.float32)

                        slots[0] = slots[0] + 1

                return carry

            lax.fori_loop(0, blocks, block, 0)
            got[first[t]] = sums[...].astype(got.dtype)
            pltpu.make_async_copy(got.at[first[t]], table_out.at[t], out_sem.at[t]).start()

        return carry

    lax.fori_loop(0, tiles_here, many, 0)

    def drain(t, carry):
        from_zero(t).wait()
        return carry

    lax.fori_loop(0, tiles_here, drain, 0)
    save_emb.wait()


def place_tiles(lists, returned, grad_emb, loss, tiles_here):
    count, tile, width = returned.shape
    smem = pl.BlockSpec(memory_space=pltpu.SMEM)
    vmem = pl.BlockSpec(memory_space=pltpu.VMEM)
    hbm = pl.BlockSpec(memory_space=pltpu.HBM)
    dma = pltpu.SemaphoreType.DMA
    return pl.pallas_call(
        place_kernel,
        out_shape=(
            jax.ShapeDtypeStruct((tiles_here, tile, width), returned.dtype),
            jax.ShapeDtypeStruct(grad_emb.shape, grad_emb.dtype),
            jax.ShapeDtypeStruct((1, 1), jnp.float32),
        ),
        in_specs=[smem, hbm, hbm, vmem],
        out_specs=(hbm, hbm, smem),
        scratch_shapes=[
            pltpu.VMEM(returned.shape, returned.dtype),
            pltpu.VMEM(grad_emb.shape, grad_emb.dtype),
            pltpu.VMEM((tile, width), returned.dtype),
            pltpu.VMEM((tile, width), jnp.float32),
            pltpu.SMEM((tiles_here,), jnp.int32),
            pltpu.SMEM((tiles_here,), jnp.int32),
            pltpu.SMEM((tiles_here,), jnp.int32),
            pltpu.SMEM((1,), jnp.int32),
            dma,
            dma,
            dma((tiles_here,)),
        ],
        compiler_params=pltpu.CompilerParams(vmem_limit_bytes=VMEM_LIMIT),
    )(lists, returned, grad_emb, loss)


def main_kernel(
    coded,
    groups,
    dp_count,
    tiles_here,
    lists,
    labels,
    emb_hbm,
    table_hbm,
    grad_hbm,
    returned,
    loss_out,
    table,
    emb,
    out_tiles,
    tiles,
    scores,
    partial,
    outgo,
    bound_in,
    bound_out,
    bound_top,
    column,
    dz,
    piece,
    ret,
    grad,
    loss_acc,
    loss_mine,
    loss_plane,
    loss_sum,
    loss_z,
    select,
    my_slot,
    back,
    table_sem,
    emb_sem,
    grad_sem,
    tile_send,
    tile_recv,
    part_send,
    part_recv,
    bound_send,
    bound_recv,
    dz_send,
    dz_recv,
    ret_send,
    ret_recv,
    own_ret_sem,
    lp_send,
    lp_recv,
    lz_send,
    lz_recv,
    *incoming,
):
    me = lax.axis_index("proto")
    z = lax.axis_index("dp")
    rows, width = emb.shape
    list_len = lists.shape[1]
    parts, cols, _ = tiles.shape
    piece_rows = TILE // parts
    chunk = CHUNK[coded]
    half = rows // 2
    chunks = half // chunk
    dz_chunks = half // DZ_CHUNK
    ratio = DZ_CHUNK // chunk
    last = dp_count - 1
    inv_scale = 1.0 / math.sqrt(D)

    barrier = pltpu.get_barrier_semaphore()
    for k in range(1, groups):
        pl.semaphore_signal(
            barrier, inc=1, device_id={"proto": lax.rem(me + k, groups)}, device_id_type=MESH
        )
    for k in range(1, dp_count):
        pl.semaphore_signal(
            barrier, inc=1, device_id={"dp": lax.rem(z + k, dp_count)}, device_id_type=MESH
        )
    load_table = pltpu.make_async_copy(table_hbm, table, table_sem)
    load_table.start()
    load_emb = pltpu.make_async_copy(emb_hbm, emb, emb_sem)
    load_emb.start()

    base = me * tiles_here
    for b in range(groups):
        local = [lists[b, j] - base for j in range(list_len)]
        mine = [(t >= 0) & (t < tiles_here) for t in local]
        low, high = jnp.int32(0), jnp.int32(0)
        for j in range(list_len):
            high = jnp.where(mine[j], local[j], high)
            back_j = list_len - 1 - j
            low = jnp.where(mine[back_j], local[back_j], low)
        select[b * CAP] = low
        select[b * CAP + 1] = high

    load_table.wait()
    for k in range(groups):
        to = lax.rem(me + k, groups)
        for t in range(CAP):
            slot = to * CAP + t
            for g in range(parts):
                block = table[select[slot], g * piece_rows : (g + 1) * piece_rows, :]
                if k == 0:
                    incoming[g][slot] = block
                else:
                    out_tiles[g, slot] = block
    pl.semaphore_wait(barrier, groups + dp_count - 2)

    def tile_copy(g, k):
        to = lax.rem(me + k, groups)
        return pltpu.make_async_remote_copy(
            src_ref=out_tiles.at[g, pl.ds(to * CAP, CAP)],
            dst_ref=incoming[g].at[pl.ds(me * CAP, CAP)],
            send_sem=tile_send.at[g, k],
            recv_sem=tile_recv.at[g, k],
            device_id={"proto": to},
            device_id_type=MESH,
        )

    for g in range(parts):
        for k in range(1, groups):
            tile_copy(g, k).start()

    ids = [lists[me, j] for j in range(list_len)]
    owner = [lax.div(t, jnp.int32(tiles_here)) for t in ids]
    flat = []
    for j in range(list_len):
        rank = jnp.int32(0)
        for i in range(j):
            rank = rank + jnp.where(owner[i] == owner[j], 1, 0)
        flat.append(owner[j] * CAP + rank)
        my_slot[j] = flat[j]
    for s in range(groups * CAP):
        at = jnp.int32(0)
        for j in range(1, list_len):
            at = jnp.where(flat[j] == s, j, at)
        back[s] = at
    lab = labels[...]
    lab_tile = lax.shift_right_logical(lab, 7)
    within = lax.bitwise_and(lab, TILE - 1)
    part_of = lax.shift_right_logical(within, int(math.log2(piece_rows)))
    where_to = part_of * cols + lax.bitwise_and(within, piece_rows - 1)
    for j in range(list_len):
        where_to = where_to + jnp.where(lab_tile == ids[j], j * piece_rows, 0)
    for i in range(rows // 128):
        column[i * 128 : (i + 1) * 128, :] = jnp.broadcast_to(where_to[i : i + 1, :], (128, 128)).T

    loss_acc[...] = jnp.zeros_like(loss_acc)
    bound_top[...] = jnp.zeros_like(bound_top)
    load_emb.wait()

    def tiles_in(g):
        for k in range(1, groups):
            tile_copy(g, k).wait()
        for j in range(list_len):
            tiles[g, j * piece_rows : (j + 1) * piece_rows, :] = incoming[g][my_slot[j]]

    def rows_of(way, at):
        return pl.multiple_of((1 - way) * half + at, 32)

    def part_copy(way, g, c, first):
        here = pl.ds(pl.multiple_of(c * chunk, chunk), chunk)
        dst = partial.at[way, g, here]
        if coded:
            src = outgo.at[way, g, here]
        elif first:
            src = scores.at[g, pl.ds(rows_of(way, c * chunk), chunk)]
        else:
            src = dst
        return pltpu.make_async_remote_copy(
            src_ref=src,
            dst_ref=dst,
            send_sem=part_send.at[way, g, c],
            recv_sem=part_recv.at[way, g, c],
            device_id={"dp": jnp.clip(z + 1 - 2 * way, 0, last)},
            device_id_type=MESH,
        )

    def bound_copy(way, g):
        return pltpu.make_async_remote_copy(
            src_ref=bound_out.at[way, g],
            dst_ref=bound_in.at[way, g],
            send_sem=bound_send.at[way, g],
            recv_sem=bound_recv.at[way, g],
            device_id={"dp": jnp.clip(z + 1 - 2 * way, 0, last)},
            device_id_type=MESH,
        )

    def dz_copy(way, u):
        at = dz.at[u // dz_chunks, pl.ds(rows_of(way, lax.rem(u, dz_chunks) * DZ_CHUNK), DZ_CHUNK)]
        return pltpu.make_async_remote_copy(
            src_ref=at,
            dst_ref=at,
            send_sem=dz_send.at[way, u],
            recv_sem=dz_recv.at[way, u],
            device_id={"dp": jnp.clip(z - 1 + 2 * way, 0, last)},
            device_id_type=MESH,
        )

    def ret_copy(q, k):
        to = lax.rem(me + k, groups)
        return pltpu.make_async_remote_copy(
            src_ref=ret.at[q, pl.ds(to * CAP, CAP)],
            dst_ref=returned.at[pl.ds(me * CAP, CAP), pl.ds(pl.multiple_of(q * piece_rows, 16), piece_rows)],
            send_sem=ret_send.at[q, k],
            recv_sem=ret_recv.at[q, k],
            device_id={"proto": to},
            device_id_type=MESH,
        )

    def own_ret(q):
        return pltpu.make_async_copy(
            ret.at[q, pl.ds(me * CAP, CAP)],
            returned.at[pl.ds(me * CAP, CAP), pl.ds(pl.multiple_of(q * piece_rows, 16), piece_rows)],
            own_ret_sem.at[q],
        )

    lane = lax.broadcasted_iota(jnp.int32, (chunk, cols), 1)

    def wide(x):
        return jnp.concatenate([x] * (cols // 128), axis=1) if cols > 128 else x

    def softmax(at):
        target_at = wide(column[at, :])
        score = [scores[g, at, :] * inv_scale for g in range(parts)]
        top = score[0]
        for g in range(1, parts):
            top = jnp.maximum(top, score[g])
        top = jnp.max(top, axis=1, keepdims=True)
        expo = [jnp.exp(s - top) for s in score]
        total = expo[0]
        for g in range(1, parts):
            total = total + expo[g]
        total = jnp.sum(total, axis=1, keepdims=True)
        scale = 1.0 / total
        target = jnp.zeros((chunk, cols), jnp.float32)
        for g in range(parts):
            onehot = lane + g * cols == target_at
            target = target + jnp.where(onehot, score[g], 0.0)
            dz[g, at, :] = (expo[g] * scale - jnp.where(onehot, 1.0, 0.0)).astype(dz.dtype)
        target = jnp.sum(target, axis=1, keepdims=True)
        loss_acc[...] += (top + jnp.log(total)) - target + jnp.zeros_like(loss_acc)

    def encode(way, g, c, value):
        here = pl.ds(pl.multiple_of(c * chunk, chunk), chunk)
        gain = wide(CODE_MAX / bound_out[way, g, 0:1, :])
        code = (value * gain + ROUND) - ROUND
        outgo[way, g, here, :] = code.astype(jnp.int32).astype(outgo.dtype)

    def decode(way, g, c):
        here = pl.ds(pl.multiple_of(c * chunk, chunk), chunk)
        if not coded:
            return partial[way, g, here, :]
        gain = wide(bound_in[way, g, 0:1, :] * (1.0 / CODE_MAX))
        return partial[way, g, here, :].astype(jnp.int32).astype(jnp.float32) * gain

    def new_block(way, g, pos):
        these = pl.ds(rows_of(way, 0), half)
        block = lax.dot_general(
            emb[these, :], tiles[g], (((1,), (1,)), ((), ())), preferred_element_type=jnp.float32
        )
        scores[g, these, :] = block
        if not coded:
            return
        biggest = jnp.max(jnp.max(jnp.abs(block), axis=0, keepdims=True), axis=1, keepdims=True)
        biggest = jnp.broadcast_to(biggest, (8, 128))

        @pl.when(pos == 0)
        def _():
            bound_out[way, g] = jnp.maximum(biggest, 1e-20)

        @pl.when(pos > 0)
        def _():
            bound_copy(way, g).wait_recv()
            bound_out[way, g] = bound_in[way, g] + biggest

        @pl.when(pos < last)
        def _():
            bound_copy(way, g).start()
            bound_top[...] = jnp.maximum(bound_top[...], bound_out[way, g])

    dz_start = (parts - 1) * chunks + LAG * last
    tail_start = ratio * dz_chunks
    ret_start = dz_start + tail_start + DZ_LAG * last
    steps = ret_start + (parts - 1) * dz_chunks + 1

    def send_pieces(q):
        out = lax.dot_general(
            dz[q], emb[...], (((0,), (0,)), ((), ())), preferred_element_type=jnp.float32
        ).astype(piece.dtype)
        for j in range(list_len):
            piece[j] = out[j * piece_rows : (j + 1) * piece_rows, :]
        for k in range(1, groups):
            to = lax.rem(me + k, groups)
            for t in range(CAP):
                ret[q, to * CAP + t] = piece[back[to * CAP + t]]
            ret_copy(q, k).start()
        for t in range(CAP):
            ret[q, me * CAP + t] = piece[back[me * CAP + t]]
        own_ret(q).start()

    def step(i, carry):
        for g in range(parts):

            @pl.when(i == 2 * g * chunks)
            def _():
                tiles_in(g)

        way = lax.rem(i, 2)
        s = i // 2
        q_step = s - ret_start

        @pl.when((way == 0) & (q_step >= 0) & (lax.rem(q_step, dz_chunks) == 0))
        def _():
            send_pieces(q_step // dz_chunks)

        pos = jnp.where(way == 0, z, last - z)
        turn = s - LAG * pos

        @pl.when((turn >= 0) & (turn < parts * chunks))
        def _():
            g = turn // chunks
            c = lax.rem(turn, chunks)

            @pl.when(c == 0)
            def _():
                new_block(way, g, pos)

            at = pl.ds(rows_of(way, c * chunk), chunk)

            @pl.when(pos == 0)
            def _():
                if coded:
                    encode(way, g, c, scores[g, at, :])
                part_copy(way, g, c, True).start()

            @pl.when((pos > 0) & (pos < last))
            def _():
                part_copy(way, g, c, False).wait_recv()
                value = decode(way, g, c) + scores[g, at, :]
                if coded:
                    encode(way, g, c, value)
                else:
                    partial[way, g, pl.ds(pl.multiple_of(c * chunk, chunk), chunk), :] = value
                part_copy(way, g, c, False).start()

            @pl.when(pos == last)
            def _():
                part_copy(way, g, c, False).wait_recv()
                scores[g, at, :] += decode(way, g, c)

            @pl.when((pos == last) & (g == parts - 1))
            def _():
                softmax(at)

        d = s - dz_start - DZ_LAG * (last - pos)
        u = jnp.where(d < tail_start, d // ratio, d - tail_start + dz_chunks)
        now = (d >= 0) & (u < parts * dz_chunks)
        now = now & ((d >= tail_start) | (lax.rem(d + ratio, ratio) == ratio - 1))

        @pl.when(now & (pos < last))
        def _():
            dz_copy(way, u).wait_recv()

        @pl.when(now & (pos > 0))
        def _():
            dz_copy(way, u).start()

        return carry

    lax.fori_loop(0, 2 * steps, step, 0)

    mine = jnp.broadcast_to(jnp.sum(loss_acc[...], axis=0, keepdims=True), (8, 128))
    too_big = jnp.where(bound_top[...] * inv_scale > 48.0, 1.0, 0.0)
    loss_mine[...] = jnp.where(lax.broadcasted_iota(jnp.int32, (8, 128), 0) < 4, mine, too_big)

    def lp_copy(k):
        return pltpu.make_async_remote_copy(
            src_ref=loss_mine,
            dst_ref=loss_plane.at[me],
            send_sem=lp_send.at[k],
            recv_sem=lp_recv.at[k],
            device_id={"proto": lax.rem(me + k, groups)},
            device_id_type=MESH,
        )

    for k in range(1, groups):
        lp_copy(k).start()

    block = 256

    def grad_block(i, carry):
        at = pl.ds(pl.multiple_of(i * block, block), block)
        total = jnp.dot(dz[0, at, :], tiles[0], preferred_element_type=jnp.float32)
        for g in range(1, parts):
            total = total + jnp.dot(dz[g, at, :], tiles[g], preferred_element_type=jnp.float32)
        grad[at, :] = total.astype(grad.dtype)
        return carry

    lax.fori_loop(0, rows // block, grad_block, 0)
    save_grad = pltpu.make_async_copy(grad, grad_hbm, grad_sem)
    save_grad.start()

    loss_plane[me] = loss_mine[...]
    for k in range(1, groups):
        lp_copy(k).wait()
    plane = loss_plane[0]
    for k in range(1, groups):
        plane = plane + loss_plane[k]
    loss_sum[...] = plane

    def lz_copy(k):
        return pltpu.make_async_remote_copy(
            src_ref=loss_sum,
            dst_ref=loss_z.at[z],
            send_sem=lz_send.at[k],
            recv_sem=lz_recv.at[k],
            device_id={"dp": lax.rem(z + k, dp_count)},
            device_id_type=MESH,
        )

    for k in range(1, dp_count):
        lz_copy(k).start()
    loss_z[z] = plane
    for k in range(1, dp_count):
        lz_copy(k).wait()
    whole = loss_z[0]
    for k in range(1, dp_count):
        whole = whole + loss_z[k]
    loss_out[...] = whole * (1.0 / (rows * groups))

    def drain_parts(i, carry):
        way = lax.rem(i, 2)
        turn = i // 2

        @pl.when(jnp.where(way == 0, z, last - z) < last)
        def _():
            part_copy(way, turn // chunks, lax.rem(turn, chunks), False).wait_send()

        return carry

    lax.fori_loop(0, 2 * parts * chunks, drain_parts, 0)

    def drain_dz(i, carry):
        way = lax.rem(i, 2)

        @pl.when(jnp.where(way == 0, z, last - z) > 0)
        def _():
            dz_copy(way, i // 2).wait_send()

        return carry

    lax.fori_loop(0, 2 * parts * dz_chunks, drain_dz, 0)
    if coded:

        def drain_bounds(i, carry):
            way = lax.rem(i, 2)

            @pl.when(jnp.where(way == 0, z, last - z) < last)
            def _():
                bound_copy(way, i // 2).wait_send()

            return carry

        lax.fori_loop(0, 2 * parts, drain_bounds, 0)
    save_grad.wait()

    def drain_ret(q, carry):
        own_ret(q).wait()
        for k in range(1, groups):
            ret_copy(q, k).wait()
        return carry

    lax.fori_loop(0, parts, drain_ret, 0)


def run_main(coded, lists, labels, embeddings, table):
    block_rows, width = embeddings.shape
    list_len = lists.shape[1]
    tiles_here = table.shape[0] // TILE
    groups = lax.axis_size("proto")
    dp_count = lax.axis_size("dp")
    slots = groups * CAP
    cols = list_len * TILE // PARTS
    piece_rows = TILE // PARTS
    half = block_rows // 2
    chunks = half // CHUNK[coded]
    dz_chunks = half // DZ_CHUNK
    bf16, f32, i32 = jnp.bfloat16, jnp.float32, jnp.int32
    dma = pltpu.SemaphoreType.DMA
    vmem = pl.BlockSpec(memory_space=pltpu.VMEM)
    smem = pl.BlockSpec(memory_space=pltpu.SMEM)
    hbm = pl.BlockSpec(memory_space=pltpu.HBM)
    wire = (2, PARTS, half, cols)
    small = (2, PARTS, 8, 128)
    return pl.pallas_call(
        functools.partial(main_kernel, coded, groups, dp_count, tiles_here),
        out_shape=(
            jax.ShapeDtypeStruct((block_rows, width), bf16),
            jax.ShapeDtypeStruct((slots, TILE, width), bf16),
            jax.ShapeDtypeStruct((8, 128), f32),
        ),
        in_specs=[smem, vmem, hbm, hbm],
        out_specs=(hbm, hbm, vmem),
        scratch_shapes=[
            pltpu.VMEM((tiles_here, TILE, width), bf16),
            pltpu.VMEM((block_rows, width), bf16),
            pltpu.VMEM((PARTS, slots, piece_rows, width), bf16),
            pltpu.VMEM((PARTS, cols, width), bf16),
            pltpu.VMEM((PARTS, block_rows, cols), f32),
            pltpu.VMEM(wire, jnp.int16 if coded else f32),
            pltpu.VMEM(wire if coded else (2, PARTS, 16, cols), jnp.int16),
            pltpu.VMEM(small, f32),
            pltpu.VMEM(small, f32),
            pltpu.VMEM((8, 128), f32),
            pltpu.VMEM((block_rows, 128), i32),
            pltpu.VMEM((PARTS, block_rows, cols), bf16),
            pltpu.VMEM((list_len, piece_rows, width), bf16),
            pltpu.VMEM((PARTS, slots, piece_rows, width), bf16),
            pltpu.VMEM((block_rows, width), bf16),
            pltpu.VMEM((CHUNK[coded], 128), f32),
            pltpu.VMEM((8, 128), f32),
            pltpu.VMEM((groups, 8, 128), f32),
            pltpu.VMEM((8, 128), f32),
            pltpu.VMEM((dp_count, 8, 128), f32),
            pltpu.SMEM((slots,), i32),
            pltpu.SMEM((list_len,), i32),
            pltpu.SMEM((slots,), i32),
            dma,
            dma,
            dma,
            dma((PARTS, groups)),
            dma((PARTS, groups)),
            dma((2, PARTS, chunks)),
            dma((2, PARTS, chunks)),
            dma((2, PARTS)),
            dma((2, PARTS)),
            dma((2, PARTS * dz_chunks)),
            dma((2, PARTS * dz_chunks)),
            dma((PARTS, groups)),
            dma((PARTS, groups)),
            dma((PARTS,)),
            dma((groups,)),
            dma((groups,)),
            dma((dp_count,)),
            dma((dp_count,)),
        ]
        + [pltpu.VMEM((slots, piece_rows, width), bf16)] * PARTS,
        compiler_params=pltpu.CompilerParams(
            collective_id=int(coded), has_side_effects=True, vmem_limit_bytes=VMEM_LIMIT
        ),
    )(lists, labels.reshape(block_rows // 128, 128), embeddings, table.reshape(tiles_here, TILE, width))


def fused_body(embeddings, table, tile_lists, labels):
    tiles_here = table.shape[0] // TILE

    def finish(grad_emb, returned, loss):
        return place_tiles(tile_lists, returned, grad_emb, loss, tiles_here)

    grad_table, grad_emb, loss = finish(*run_main(CODED, tile_lists, labels, embeddings, table))
    return (loss.reshape(()), grad_emb, grad_table.reshape(table.shape))


def any_body(embeddings, table, tile_lists, labels):
    block_rows, width = embeddings.shape
    cols = tile_lists.shape[1] * TILE
    need = block_rows * cols * (4 + 4 + 2 + 2) + 2 * table.shape[0] * width * 2
    if need + 8 * 2**20 <= VMEM_LIMIT and block_rows % 1024 == 0:
        return fused_body(embeddings, table, tile_lists, labels)
    return body(embeddings, table, tile_lists, labels)


def solution(mesh):
    placed = (P("proto", "dp"), P("proto", "dp"), P(), P("proto"))
    return jax.shard_map(
        any_body,
        mesh=mesh,
        in_specs=placed,
        out_specs=(P(), P("proto", "dp"), P("proto", "dp")),
        check_vma=False,
    )
```

time: 164 us -> 129 us (0.79)
  Pallas kernels: 146 us -> 128 us
  local copies, waits for them, and re-layouts: 10.3 us -> 0 us
  other arithmetic: 4.2 us -> 0 us
  between operations: 2.5 us -> 0.64 us
    pallas_call x3 -> x2, Pallas kernels: 146 us -> 128 us  [the longest x1 122 us: run_main(): pl.pallas_call(functools.partial(main_kernel, coded, groups, dp_count, ti...]
    unnamed x10 -> x0, local copies, waits for them, and re-layouts: 7.03 us -> none
where the time goes in v1:
time: 129 us
  Pallas kernels  128 us (99%)
    pallas_call x1, Pallas kernels, run_main(): pl.pallas_call(functools.partial(main_kernel, coded, groups, dp_count, ti...  122 us
    pallas_call x1, Pallas kernels, place_tiles(): pl.pallas_call(place_kernel, out_shape=(jax.ShapeDtypeStruct((tiles_here,...  6.23 us

profile of v1, /device:TPU:0, one launch (start us, length us, event | category | flops | bytes accessed | tf_op | source)
XLA Modules:
  0.0 128.8 jit_solution(12215220824107964579)
XLA Ops:
  0.6 121.9 %shard_map.67 = (bf16[1024,640]{1,0:T(8,128)(2,1)}, bf16[16,128,640]{2,1,0:T(8,128)(2,1)}, f32[8,128]{1,0:T(8,128)}) custom-call(s32[8,8]{1,0:T(8,128)} %lists.3, s32[8,128]{1,0:T(8,128)} %bitcast.5, bf16[1024,640]{1,0:T(8,128)(2,1)} %emb_hbm.1, bf16[32,128,640]{2,1,0:T(8,128)(2,1)} %bitcast.4), custom_call_target="tpu_custom_call" | custom-call | tf_op jit(solution)/shard_map/pallas_call | solution.py:780
  122.6 6.2 %shard_map.68 = (bf16[32,128,640]{2,1,0:T(8,128)(2,1)}, bf16[1024,640]{1,0:T(8,128)(2,1)}, f32[1,1]{1,0:T(1,128)}) custom-call(s32[8,8]{1,0:T(8,128)} %lists.3, bf16[16,128,640]{2,1,0:T(8,128)(2,1)} %get-tuple-element.9.returned, bf16[1024,640]{1,0:T(8,128)(2,1)} %get-tuple-element.10.emb_in, f32[8,128]{1,0:T(8,128)} %get-tuple-element.11.loss_in), custom_call_target="tpu_custom_call" | custom-call | tf_op jit(solution)/shard_map/pallas_call | solution.py:259

commit v2 on v1

--- a/solution.py
+++ b/solution.py
@@ -12,12 +12,14 @@
 TILE = 128
 CAP = 2
 PARTS = 4
-CHUNK = {False: 32, True: 64}
-DZ_CHUNK = 64
+CHUNK = {False: 64, True: 128}
+DZ_CHUNK = 128
 LAG = 4
 DZ_LAG = 4
-CODED = False
 CODE_MAX = 32766.0
+GUARD = 1
+BOUND = 48.0
+SOFT = 32
 ROUND = 12582912.0
 VMEM_LIMIT = 56 * 2**20
 MESH = pl.DeviceIdType.MESH
@@ -147,110 +149,70 @@
     )(pick, shaped_table)
 
 
-def place_kernel(lists, returned, emb_in, loss_in, table_out, emb_out, loss_out, got, emb, zero, sums, count, first, second, slots, in_sem, emb_sem, out_sem):
-    me = lax.axis_index("proto")
-    blocks, list_len = lists.shape
+def place_kernel(plan, returned, emb_in, loss_in, table_out, emb_out, loss_out, got, emb, zero, sums, in_sem, emb_sem, out_sem):
     tiles_here = table_out.shape[0]
+    count = returned.shape[0]
     load = pltpu.make_async_copy(returned, got, in_sem)
     load.start()
     load_emb = pltpu.make_async_copy(emb_in, emb, emb_sem)
     load_emb.start()
     zero[...] = jnp.zeros_like(zero)
-    base = me * tiles_here
-
-    def clear(t, carry):
-        count[t] = 0
-        first[t] = 0
-        return carry
-
-    lax.fori_loop(0, tiles_here, clear, 0)
-
-    def note(b, carry):
-        slots[0] = b * CAP
-        for j in range(list_len):
-            tile = lists[b, j] - base
-
-            @pl.when((tile >= 0) & (tile < tiles_here))
-            def _():
-                seen = count[tile]
-                second[tile] = first[tile]
-                first[tile] = slots[0]
-                count[tile] = seen + 1
-                slots[0] = slots[0] + 1
-
-        return carry
-
-    lax.fori_loop(0, blocks, note, 0)
 
     def from_zero(t):
         return pltpu.make_async_copy(zero, table_out.at[t], out_sem.at[t])
 
-    def zeros(t, carry):
-        @pl.when(count[t] == 0)
+    def from_slot(t):
+        return pltpu.make_async_copy(got.at[plan[1, t]], table_out.at[t], out_sem.at[t])
+
+    for t in range(tiles_here):
+
+        @pl.when(plan[0, t] == 0)
         def _():
             from_zero(t).start()
 
-        return carry
-
-    lax.fori_loop(0, tiles_here, zeros, 0)
-    loss_out[0, 0] = jnp.max(loss_in[0:1, :])
     load_emb.wait()
     save_emb = pltpu.make_async_copy(emb, emb_out, emb_sem)
     save_emb.start()
     load.wait()
-
-    def ones(t, carry):
-        @pl.when(count[t] == 1)
-        def _():
-            pltpu.make_async_copy(got.at[first[t]], table_out.at[t], out_sem.at[t]).start()
+    for t in range(tiles_here):
+
+        @pl.when(plan[0, t] == 1)
+        def _():
+            from_slot(t).start()
+
+    def many(t, carry):
+        @pl.when(plan[0, t] == 2)
+        def _():
+            sums[...] = got[plan[1, t]].astype(jnp.float32) + got[plan[2, t]].astype(jnp.float32)
+
+        @pl.when(plan[0, t] > 2)
+        def _():
+            sums[...] = jnp.zeros_like(sums)
+
+            def add(slot, carry):
+                @pl.when(plan[3, slot] == t)
+                def _():
+                    sums[...] += got[slot].astype(jnp.float32)
+
+                return carry
+
+            lax.fori_loop(0, count, add, 0)
+
+        @pl.when(plan[0, t] > 1)
+        def _():
+            got[plan[1, t]] = sums[...].astype(got.dtype)
+            from_slot(t).start()
 
         return carry
 
-    lax.fori_loop(0, tiles_here, ones, 0)
-
-    def many(t, carry):
-        @pl.when(count[t] == 2)
-        def _():
-            total = got[first[t]].astype(jnp.float32) + got[second[t]].astype(jnp.float32)
-            got[first[t]] = total.astype(got.dtype)
-            pltpu.make_async_copy(got.at[first[t]], table_out.at[t], out_sem.at[t]).start()
-
-        @pl.when(count[t] > 2)
-        def _():
-            sums[...] = jnp.zeros_like(sums)
-
-            def block(b, carry):
-                slots[0] = b * CAP
-                for j in range(list_len):
-                    tile = lists[b, j] - base
-
-                    @pl.when((tile >= 0) & (tile < tiles_here))
-                    def _():
-                        @pl.when(tile == t)
-                        def _():
-                            sums[...] += got[slots[0]].astype(jnp.float32)
-
-                        slots[0] = slots[0] + 1
-
-                return carry
-
-            lax.fori_loop(0, blocks, block, 0)
-            got[first[t]] = sums[...].astype(got.dtype)
-            pltpu.make_async_copy(got.at[first[t]], table_out.at[t], out_sem.at[t]).start()
-
-        return carry
-
     lax.fori_loop(0, tiles_here, many, 0)
-
-    def drain(t, carry):
+    loss_out[0, 0] = jnp.max(loss_in[0:1, :])
+    for t in range(tiles_here):
         from_zero(t).wait()
-        return carry
-
-    lax.fori_loop(0, tiles_here, drain, 0)
     save_emb.wait()
 
 
-def place_tiles(lists, returned, grad_emb, loss, tiles_here):
+def place_tiles(plan, returned, grad_emb, loss, tiles_here):
     count, tile, width = returned.shape
     smem = pl.BlockSpec(memory_space=pltpu.SMEM)
     vmem = pl.BlockSpec(memory_space=pltpu.VMEM)
@@ -270,16 +232,12 @@
             pltpu.VMEM(grad_emb.shape, grad_emb.dtype),
             pltpu.VMEM((tile, width), returned.dtype),
             pltpu.VMEM((tile, width), jnp.float32),
-            pltpu.SMEM((tiles_here,), jnp.int32),
-            pltpu.SMEM((tiles_here,), jnp.int32),
-            pltpu.SMEM((tiles_here,), jnp.int32),
-            pltpu.SMEM((1,), jnp.int32),
             dma,
             dma,
             dma((tiles_here,)),
         ],
         compiler_params=pltpu.CompilerParams(vmem_limit_bytes=VMEM_LIMIT),
-    )(lists, returned, grad_emb, loss)
+    )(plan, returned, grad_emb, loss)
 
 
 def main_kernel(
@@ -294,6 +252,7 @@
     grad_hbm,
     returned,
     loss_out,
+    plan_out,
     table,
     emb,
     out_tiles,
@@ -303,6 +262,7 @@
     outgo,
     bound_in,
     bound_out,
+    bound_own,
     bound_top,
     column,
     dz,
@@ -349,6 +309,7 @@
     dz_chunks = half // DZ_CHUNK
     ratio = DZ_CHUNK // chunk
     last = dp_count - 1
+    block = 256
     inv_scale = 1.0 / math.sqrt(D)
 
     barrier = pltpu.get_barrier_semaphore()
@@ -366,6 +327,9 @@
     load_emb.start()
 
     base = me * tiles_here
+    lane_one = lax.broadcasted_iota(jnp.int32, (1, 128), 1)
+    count = jnp.zeros((1, 128), jnp.int32)
+    first, second, held = count, count, count
     for b in range(groups):
         local = [lists[b, j] - base for j in range(list_len)]
         mine = [(t >= 0) & (t < tiles_here) for t in local]
@@ -376,6 +340,22 @@
             low = jnp.where(mine[back_j], local[back_j], low)
         select[b * CAP] = low
         select[b * CAP + 1] = high
+        listed = mine[0]
+        for j in range(1, list_len):
+            listed = listed | mine[j]
+        for t, tile in enumerate((low, high)):
+            slot = b * CAP + t
+            tile = jnp.where(listed, tile, -1)
+            hit = lane_one == tile
+            count = count + jnp.where(hit, 1, 0)
+            second = jnp.where(hit, first, second)
+            first = jnp.where(hit, slot, first)
+            held = jnp.where(lane_one == slot, tile, held)
+    plan_out[0:1, :] = count
+    plan_out[1:2, :] = first
+    plan_out[2:3, :] = second
+    plan_out[3:4, :] = held
+    plan_out[4:8, :] = jnp.zeros((4, 128), jnp.int32)
 
     load_table.wait()
     for k in range(groups):
@@ -383,11 +363,11 @@
         for t in range(CAP):
             slot = to * CAP + t
             for g in range(parts):
-                block = table[select[slot], g * piece_rows : (g + 1) * piece_rows, :]
+                tile = table[select[slot], g * piece_rows : (g + 1) * piece_rows, :]
                 if k == 0:
-                    incoming[g][slot] = block
+                    incoming[g][slot] = tile
                 else:
-                    out_tiles[g, slot] = block
+                    out_tiles[g, slot] = tile
     pl.semaphore_wait(barrier, groups + dp_count - 2)
 
     def tile_copy(g, k):
@@ -401,9 +381,18 @@
             device_id_type=MESH,
         )
 
-    for g in range(parts):
-        for k in range(1, groups):
-            tile_copy(g, k).start()
+    core = lax.rem(me, 2)
+    for first in range(2):
+        for g in range(parts):
+            for a in range(groups // 2):
+                k = lax.rem(2 * a + first - core + groups, groups)
+                if a > 0:
+                    tile_copy(g, k).start()
+                else:
+
+                    @pl.when(core != first)
+                    def _():
+                        tile_copy(g, k).start()
 
     ids = [lists[me, j] for j in range(list_len)]
     owner = [lax.div(t, jnp.int32(tiles_here)) for t in ids]
@@ -435,7 +424,7 @@
 
     def tiles_in(g):
         for k in range(1, groups):
-            tile_copy(g, k).wait()
+            tile_copy(g, k).wait_recv()
         for j in range(list_len):
             tiles[g, j * piece_rows : (j + 1) * piece_rows, :] = incoming[g][my_slot[j]]
 
@@ -499,12 +488,13 @@
             own_ret_sem.at[q],
         )
 
-    lane = lax.broadcasted_iota(jnp.int32, (chunk, cols), 1)
+    lane = lax.broadcasted_iota(jnp.int32, (SOFT, cols), 1)
 
     def wide(x):
         return jnp.concatenate([x] * (cols // 128), axis=1) if cols > 128 else x
 
-    def softmax(at):
+    def softmax_rows(i, start):
+        at = pl.ds(pl.multiple_of(start + i * SOFT, SOFT), SOFT)
         target_at = wide(column[at, :])
         score = [scores[g, at, :] * inv_scale for g in range(parts)]
         top = score[0]
@@ -517,13 +507,14 @@
             total = total + expo[g]
         total = jnp.sum(total, axis=1, keepdims=True)
         scale = 1.0 / total
-        target = jnp.zeros((chunk, cols), jnp.float32)
+        target = jnp.zeros((SOFT, cols), jnp.float32)
         for g in range(parts):
             onehot = lane + g * cols == target_at
             target = target + jnp.where(onehot, score[g], 0.0)
             dz[g, at, :] = (expo[g] * scale - jnp.where(onehot, 1.0, 0.0)).astype(dz.dtype)
         target = jnp.sum(target, axis=1, keepdims=True)
         loss_acc[...] += (top + jnp.log(total)) - target + jnp.zeros_like(loss_acc)
+        return start
 
     def encode(way, g, c, value):
         here = pl.ds(pl.multiple_of(c * chunk, chunk), chunk)
@@ -538,25 +529,35 @@
         gain = wide(bound_in[way, g, 0:1, :] * (1.0 / CODE_MAX))
         return partial[way, g, here, :].astype(jnp.int32).astype(jnp.float32) * gain
 
-    def new_block(way, g, pos):
-        these = pl.ds(rows_of(way, 0), half)
-        block = lax.dot_general(
-            emb[these, :], tiles[g], (((1,), (1,)), ((), ())), preferred_element_type=jnp.float32
-        )
-        scores[g, these, :] = block
-        if not coded:
-            return
-        biggest = jnp.max(jnp.max(jnp.abs(block), axis=0, keepdims=True), axis=1, keepdims=True)
-        biggest = jnp.broadcast_to(biggest, (8, 128))
-
+    def new_block(g):
+        biggest = []
+        for r in range(rows // block):
+            these = slice(r * block, (r + 1) * block)
+            value = lax.dot_general(
+                emb[these, :], tiles[g], (((1,), (1,)), ((), ())), preferred_element_type=jnp.float32
+            )
+            scores[g, these, :] = value
+            if coded:
+                biggest.append(jnp.max(jnp.abs(value), axis=0, keepdims=True))
+        if coded:
+            per_way = len(biggest) // 2
+            for way in range(2):
+                some = biggest[(1 - way) * per_way : (2 - way) * per_way]
+                top = some[0]
+                for x in some[1:]:
+                    top = jnp.maximum(top, x)
+                top = jnp.max(top, axis=1, keepdims=True)
+                bound_own[way, g] = jnp.broadcast_to(jnp.maximum(top, 1e-20), (8, 128))
+
+    def new_bound(way, g, pos):
         @pl.when(pos == 0)
         def _():
-            bound_out[way, g] = jnp.maximum(biggest, 1e-20)
+            bound_out[way, g] = bound_own[way, g]
 
         @pl.when(pos > 0)
         def _():
             bound_copy(way, g).wait_recv()
-            bound_out[way, g] = bound_in[way, g] + biggest
+            bound_out[way, g] = bound_in[way, g] + bound_own[way, g]
 
         @pl.when(pos < last)
         def _():
@@ -583,6 +584,53 @@
             ret[q, me * CAP + t] = piece[back[me * CAP + t]]
         own_ret(q).start()
 
+    def lp_copy(k):
+        return pltpu.make_async_remote_copy(
+            src_ref=loss_mine,
+            dst_ref=loss_plane.at[me],
+            send_sem=lp_send.at[k],
+            recv_sem=lp_recv.at[k],
+            device_id={"proto": lax.rem(me + k, groups)},
+            device_id_type=MESH,
+        )
+
+    def lz_copy(k):
+        return pltpu.make_async_remote_copy(
+            src_ref=loss_sum,
+            dst_ref=loss_z.at[z],
+            send_sem=lz_send.at[k],
+            recv_sem=lz_recv.at[k],
+            device_id={"dp": lax.rem(z + k, dp_count)},
+            device_id_type=MESH,
+        )
+
+    def loss_begin():
+        mine = jnp.broadcast_to(jnp.sum(loss_acc[...], axis=0, keepdims=True), (8, 128))
+        too_big = jnp.where(bound_top[...] * inv_scale > BOUND, 1.0, 0.0)
+        loss_mine[...] = jnp.where(lax.broadcasted_iota(jnp.int32, (8, 128), 0) < 4, mine, too_big)
+        loss_plane[me] = loss_mine[...]
+        for k in range(1, groups):
+            lp_copy(k).start()
+
+    def loss_middle():
+        for k in range(1, groups):
+            lp_copy(k).wait()
+        plane = loss_plane[0]
+        for k in range(1, groups):
+            plane = plane + loss_plane[k]
+        loss_sum[...] = plane
+        loss_z[z] = plane
+        for k in range(1, dp_count):
+            lz_copy(k).start()
+
+    def loss_end():
+        for k in range(1, dp_count):
+            lz_copy(k).wait()
+        whole = loss_z[0]
+        for k in range(1, dp_count):
+            whole = whole + loss_z[k]
+        loss_out[...] = whole * (1.0 / (rows * groups))
+
     def step(i, carry):
         for g in range(parts):
 
@@ -592,11 +640,22 @@
 
         way = lax.rem(i, 2)
         s = i // 2
+
+        @pl.when((way == 0) & (s < parts * chunks) & (lax.rem(s, chunks) == 0))
+        def _():
+            new_block(s // chunks)
+
         q_step = s - ret_start
 
         @pl.when((way == 0) & (q_step >= 0) & (lax.rem(q_step, dz_chunks) == 0))
         def _():
             send_pieces(q_step // dz_chunks)
+
+        for at, part in enumerate((loss_begin, loss_middle, loss_end)):
+
+            @pl.when((way == 0) & (q_step == at * dz_chunks))
+            def _():
+                part()
 
         pos = jnp.where(way == 0, z, last - z)
         turn = s - LAG * pos
@@ -606,9 +665,11 @@
             g = turn // chunks
             c = lax.rem(turn, chunks)
 
-            @pl.when(c == 0)
-            def _():
-                new_block(way, g, pos)
+            if coded:
+
+                @pl.when(c == 0)
+                def _():
+                    new_bound(way, g, pos)
 
             at = pl.ds(rows_of(way, c * chunk), chunk)
 
@@ -635,7 +696,7 @@
 
             @pl.when((pos == last) & (g == parts - 1))
             def _():
-                softmax(at)
+                lax.fori_loop(0, chunk // SOFT, softmax_rows, rows_of(way, c * chunk))
 
         d = s - dz_start - DZ_LAG * (last - pos)
         u = jnp.where(d < tail_start, d // ratio, d - tail_start + dz_chunks)
@@ -654,24 +715,9 @@
 
     lax.fori_loop(0, 2 * steps, step, 0)
 
-    mine = jnp.broadcast_to(jnp.sum(loss_acc[...], axis=0, keepdims=True), (8, 128))
-    too_big = jnp.where(bound_top[...] * inv_scale > 48.0, 1.0, 0.0)
-    loss_mine[...] = jnp.where(lax.broadcasted_iota(jnp.int32, (8, 128), 0) < 4, mine, too_big)
-
-    def lp_copy(k):
-        return pltpu.make_async_remote_copy(
-            src_ref=loss_mine,
-            dst_ref=loss_plane.at[me],
-            send_sem=lp_send.at[k],
-            recv_sem=lp_recv.at[k],
-            device_id={"proto": lax.rem(me + k, groups)},
-            device_id_type=MESH,
-        )
-
-    for k in range(1, groups):
-        lp_copy(k).start()
-
-    block = 256
+    def save_grad(i):
+        at = pl.ds(pl.multiple_of(i * block, block), block)
+        return pltpu.make_async_copy(grad.at[at], grad_hbm.at[at], grad_sem.at[i])
 
     def grad_block(i, carry):
         at = pl.ds(pl.multiple_of(i * block, block), block)
@@ -679,39 +725,10 @@
         for g in range(1, parts):
             total = total + jnp.dot(dz[g, at, :], tiles[g], preferred_element_type=jnp.float32)
         grad[at, :] = total.astype(grad.dtype)
+        save_grad(i).start()
         return carry
 
     lax.fori_loop(0, rows // block, grad_block, 0)
-    save_grad = pltpu.make_async_copy(grad, grad_hbm, grad_sem)
-    save_grad.start()
-
-    loss_plane[me] = loss_mine[...]
-    for k in range(1, groups):
-        lp_copy(k).wait()
-    plane = loss_plane[0]
-    for k in range(1, groups):
-        plane = plane + loss_plane[k]
-    loss_sum[...] = plane
-
-    def lz_copy(k):
-        return pltpu.make_async_remote_copy(
-            src_ref=loss_sum,
-            dst_ref=loss_z.at[z],
-            send_sem=lz_send.at[k],
-            recv_sem=lz_recv.at[k],
-            device_id={"dp": lax.rem(z + k, dp_count)},
-            device_id_type=MESH,
-        )
-
-    for k in range(1, dp_count):
-        lz_copy(k).start()
-    loss_z[z] = plane
-    for k in range(1, dp_count):
-        lz_copy(k).wait()
-    whole = loss_z[0]
-    for k in range(1, dp_count):
-        whole = whole + loss_z[k]
-    loss_out[...] = whole * (1.0 / (rows * groups))
 
     def drain_parts(i, carry):
         way = lax.rem(i, 2)
@@ -747,7 +764,11 @@
             return carry
 
         lax.fori_loop(0, 2 * parts, drain_bounds, 0)
-    save_grad.wait()
+    for g in range(parts):
+        for k in range(1, groups):
+            tile_copy(g, k).wait_send()
+    for i in range(rows // block):
+        save_grad(i).wait()
 
     def drain_ret(q, carry):
         own_ret(q).wait()
@@ -783,9 +804,10 @@
             jax.ShapeDtypeStruct((block_rows, width), bf16),
             jax.ShapeDtypeStruct((slots, TILE, width), bf16),
             jax.ShapeDtypeStruct((8, 128), f32),
+            jax.ShapeDtypeStruct((8, 128), i32),
         ),
         in_specs=[smem, vmem, hbm, hbm],
-        out_specs=(hbm, hbm, vmem),
+        out_specs=(hbm, hbm, vmem, vmem),
         scratch_shapes=[
             pltpu.VMEM((tiles_here, TILE, width), bf16),
             pltpu.VMEM((block_rows, width), bf16),
@@ -796,13 +818,14 @@
             pltpu.VMEM(wire if coded else (2, PARTS, 16, cols), jnp.int16),
             pltpu.VMEM(small, f32),
             pltpu.VMEM(small, f32),
+            pltpu.VMEM(small, f32),
             pltpu.VMEM((8, 128), f32),
             pltpu.VMEM((block_rows, 128), i32),
             pltpu.VMEM((PARTS, block_rows, cols), bf16),
             pltpu.VMEM((list_len, piece_rows, width), bf16),
             pltpu.VMEM((PARTS, slots, piece_rows, width), bf16),
             pltpu.VMEM((block_rows, width), bf16),
-            pltpu.VMEM((CHUNK[coded], 128), f32),
+            pltpu.VMEM((SOFT, 128), f32),
             pltpu.VMEM((8, 128), f32),
             pltpu.VMEM((groups, 8, 128), f32),
             pltpu.VMEM((8, 128), f32),
@@ -812,7 +835,7 @@
             pltpu.SMEM((slots,), i32),
             dma,
             dma,
-            dma,
+            dma((block_rows // 256,)),
             dma((PARTS, groups)),
             dma((PARTS, groups)),
             dma((2, PARTS, chunks)),
@@ -838,11 +861,22 @@
 
 def fused_body(embeddings, table, tile_lists, labels):
     tiles_here = table.shape[0] // TILE
-
-    def finish(grad_emb, returned, loss):
-        return place_tiles(tile_lists, returned, grad_emb, loss, tiles_here)
-
-    grad_table, grad_emb, loss = finish(*run_main(CODED, tile_lists, labels, embeddings, table))
+    inputs = (tile_lists, labels, embeddings, table)
+
+    def finish(grad_emb, returned, loss, plan):
+        return place_tiles(plan, returned, grad_emb, loss, tiles_here)
+
+    if GUARD == 0:
+        grad_table, grad_emb, loss = finish(*run_main(True, *inputs))
+    else:
+        coded = run_main(True, *inputs)
+        grad_table, grad_emb, loss = lax.cond(
+            coded[2][7, 0] > 0.0,
+            lambda coded, inputs: finish(*run_main(False, *inputs)),
+            lambda coded, inputs: finish(*coded),
+            coded,
+            inputs,
+        )
     return (loss.reshape(()), grad_emb, grad_table.reshape(table.shape))
 
 

time: 129 us -> 210 us (1.63)
  Pallas kernels: 128 us -> 208 us
    pallas_call x1 -> x2, Pallas kernels: 122 us -> 201 us  [run_main(): pl.pallas_call(functools.partial(main_kernel, coded, groups, dp_count, ti...]
where the time goes in v2:
time: 210 us
  Pallas kernels  208 us (99%)
    pallas_call x2, Pallas kernels, run_main(): pl.pallas_call(functools.partial(main_kernel, coded, groups, dp_count, ti...  201 us
    pallas_call x1, Pallas kernels, place_tiles(): pl.pallas_call(place_kernel, out_shape=(jax.ShapeDtypeStruct((tiles_here,...  6.56 us

profile of v2, /device:TPU:0, one launch (start us, length us, event | category | flops | bytes accessed | tf_op | source)
XLA Modules:
  0.0 209.6 jit_solution(10865870358826922382)
XLA Ops:
  0.6 0.0 copy-start
  0.6 0.0 copy-start.1
  0.7 0.0 copy-start.2
  0.7 0.0 copy-start.3
  0.7 92.1 %shard_map.67 = (bf16[1024,640]{1,0:T(8,128)(2,1)S(1)}, bf16[16,128,640]{2,1,0:T(8,128)(2,1)}, f32[8,128]{1,0:T(8,128)S(1)}, s32[8,128]{1,0:T(8,128)S(1)}) custom-call(s32[8,8]{1,0:T(8,128)} %lists.1, s32[8,128]{1,0:T(8,128)} %bitcast.11, bf16[1024,640]{1,0:T(8,128)(2,1)} %emb_hbm.1, bf16[32,128,640]{2,1,0:T(8,128)(2,1)} %bitcast.9), custom_call_target="tpu_custom_call" | custom-call | tf_op jit(solution)/shard_map/pallas_call | solution.py:801
  92.8 0.5 slice.3
  93.9 0.0 copy-done
  94.0 0.0 copy-done.1
  94.0 0.0 copy-done.2
  94.0 0.0 copy-done.3
  94.0 115.6 %conditional.1 = (bf16[1024,640]{1,0:T(8,128)(2,1)}, bf16[4096,640]{1,0:T(8,128)(2,1)}, f32[]{:T(128)}) conditional(s32[]{:T(128)} %bitcast.8, (s32[8,128]{1,0:T(8,128)S(1)}, bf16[16,128,640]{2,1,0:T(8,128)(2,1)}, bf16[1024,640]{1,0:T(8,128)(2,1)S(1)}, f32[8,128]{1,0:T(8,128)S(1)}) %tuple.20, (s32[1024]{0:T(1024)S(1)}, ...), branch_computations={%region_0.0_spmd, %region_1.0_spmd} | conditional | bytes 24 | solution.py:873
  94.0 109.0 %branch_1_fun.2 = (bf16[1024,640]{1,0:T(8,128)(2,1)}, bf16[16,128,640]{2,1,0:T(8,128)(2,1)}, f32[8,128]{1,0:T(8,128)}, s32[8,128]{1,0:T(8,128)}) custom-call(s32[8,8]{1,0:T(8,128)S(1)} %get-tuple-element.31.lists, s32[8,128]{1,0:T(8,128)S(1)} %bitcast.12, bf16[1024,640]{1,0:T(8,128)(2,1)S(1)} %get-tuple-element.33.emb_hbm, bf16[32,128,640]{2,1,0:T(8,128)(2,1)S(1)} %bitcast.10), custom_call_target="tpu_custom_call" | custom-call | tf_op jit(solution)/shard_map/cond/branch_1_fun/pallas_call | solution.py:801
  203.0 6.6 %branch_1_fun.3 = (bf16[32,128,640]{2,1,0:T(8,128)(2,1)}, bf16[1024,640]{1,0:T(8,128)(2,1)}, f32[1,1]{1,0:T(1,128)}) custom-call(s32[8,128]{1,0:T(8,128)} %get-tuple-element.35.plan, bf16[16,128,640]{2,1,0:T(8,128)(2,1)} %get-tuple-element.36.returned, bf16[1024,640]{1,0:T(8,128)(2,1)} %get-tuple-element.37.emb_in, f32[8,128]{1,0:T(8,128)} %get-tuple-element.38.loss_in), custom_call_target="tpu_custom_call" | custom-call | tf_op jit(solution)/shard_map/cond/branch_1_fun/pallas_call | solution.py:221
Async XLA Ops:
  0.6 93.3 %copy-start = (bf16[4096,640]{1,0:T(8,128)(2,1)S(1)}, bf16[4096,640]{1,0:T(8,128)(2,1)}, u32[]{:S(2)}) copy-start(bf16[4096,640]{1,0:T(8,128)(2,1)} %param.7) | copy-start | bytes 15728644
  0.6 93.3 %copy-start.1 = (bf16[1024,640]{1,0:T(8,128)(2,1)S(1)}, bf16[1024,640]{1,0:T(8,128)(2,1)}, u32[]{:S(2)}) copy-start(bf16[1024,640]{1,0:T(8,128)(2,1)} %emb_hbm.1) | copy-start | bytes 3932164
  0.7 93.3 %copy-start.2 = (s32[8,8]{1,0:T(8,128)S(1)}, s32[8,8]{1,0:T(8,128)}, u32[]{:S(2)}) copy-start(s32[8,8]{1,0:T(8,128)} %lists.1) | copy-start | bytes 772
  0.7 93.3 %copy-start.3 = (s32[1024]{0:T(1024)S(1)}, s32[1024]{0:T(1024)}, u32[]{:S(2)}) copy-start(s32[1024]{0:T(1024)} %param.9) | copy-start | bytes 12292

commit v3 on v2

--- a/solution.py
+++ b/solution.py
@@ -11,9 +11,9 @@
 D = 2560
 TILE = 128
 CAP = 2
-PARTS = 4
-CHUNK = {False: 64, True: 128}
-DZ_CHUNK = 128
+PARTS = 8
+CHUNK = {False: 64, True: 256}
+DZ_CHUNK = 256
 LAG = 4
 DZ_LAG = 4
 CODE_MAX = 32766.0
@@ -566,8 +566,7 @@
 
     dz_start = (parts - 1) * chunks + LAG * last
     tail_start = ratio * dz_chunks
-    ret_start = dz_start + tail_start + DZ_LAG * last
-    steps = ret_start + (parts - 1) * dz_chunks + 1
+    ret_start = -(-(dz_start + tail_start + DZ_LAG * last) // dz_chunks) * dz_chunks
 
     def send_pieces(q):
         out = lax.dot_general(
@@ -631,32 +630,28 @@
             whole = whole + loss_z[k]
         loss_out[...] = whole * (1.0 / (rows * groups))
 
-    def step(i, carry):
-        for g in range(parts):
-
-            @pl.when(i == 2 * g * chunks)
-            def _():
-                tiles_in(g)
-
+    def events(at):
+        @pl.when((at < parts * chunks) & (lax.rem(at, chunks) == 0))
+        def _():
+            for g in range(parts):
+
+                @pl.when(at == g * chunks)
+                def _():
+                    tiles_in(g)
+
+            new_block(at // chunks)
+
+        @pl.when(at == ret_start)
+        def _():
+            loss_begin()
+
+        @pl.when(at >= ret_start)
+        def _():
+            send_pieces((at - ret_start) // dz_chunks)
+
+    def step(i, at):
         way = lax.rem(i, 2)
-        s = i // 2
-
-        @pl.when((way == 0) & (s < parts * chunks) & (lax.rem(s, chunks) == 0))
-        def _():
-            new_block(s // chunks)
-
-        q_step = s - ret_start
-
-        @pl.when((way == 0) & (q_step >= 0) & (lax.rem(q_step, dz_chunks) == 0))
-        def _():
-            send_pieces(q_step // dz_chunks)
-
-        for at, part in enumerate((loss_begin, loss_middle, loss_end)):
-
-            @pl.when((way == 0) & (q_step == at * dz_chunks))
-            def _():
-                part()
-
+        s = at + i // 2
         pos = jnp.where(way == 0, z, last - z)
         turn = s - LAG * pos
 
@@ -711,9 +706,17 @@
         def _():
             dz_copy(way, u).start()
 
+        return at
+
+    def stage(j, carry):
+        at = j * dz_chunks
+        events(at)
+        lax.fori_loop(0, 2 * dz_chunks, step, at)
         return carry
 
-    lax.fori_loop(0, 2 * steps, step, 0)
+    lax.fori_loop(0, ret_start // dz_chunks + parts - 1, stage, 0)
+    events(jnp.int32(ret_start + (parts - 1) * dz_chunks))
+    loss_middle()
 
     def save_grad(i):
         at = pl.ds(pl.multiple_of(i * block, block), block)
@@ -729,6 +732,8 @@
         return carry
 
     lax.fori_loop(0, rows // block, grad_block, 0)
+
+    loss_end()
 
     def drain_parts(i, carry):
         way = lax.rem(i, 2)

time: 210 us -> 210 us (level)
  no operation moved by 1% of the time
where the time goes in v3:
time: 210 us; the launch traced here: 208 us
  Pallas kernels  206 us (98%)
    pallas_call x2, Pallas kernels, run_main(): pl.pallas_call(functools.partial(main_kernel, coded, groups, dp_count, ti...  199 us
    pallas_call x1, Pallas kernels, place_tiles(): pl.pallas_call(place_kernel, out_shape=(jax.ShapeDtypeStruct((tiles_here,...  6.59 us

profile of v3, /device:TPU:0, one launch (start us, length us, event | category | flops | bytes accessed | tf_op | source)
XLA Modules:
  0.0 207.8 jit_solution(11866907728398910706)
XLA Ops:
  0.6 0.0 copy-start
  0.6 0.0 copy-start.1
  0.7 0.0 copy-start.2
  0.7 0.0 copy-start.3
  0.7 85.8 %shard_map.67 = (bf16[1024,640]{1,0:T(8,128)(2,1)S(1)}, bf16[16,128,640]{2,1,0:T(8,128)(2,1)}, f32[8,128]{1,0:T(8,128)S(1)}, s32[8,128]{1,0:T(8,128)S(1)}) custom-call(s32[8,8]{1,0:T(8,128)} %lists.1, s32[8,128]{1,0:T(8,128)} %bitcast.11, bf16[1024,640]{1,0:T(8,128)(2,1)} %emb_hbm.1, bf16[32,128,640]{2,1,0:T(8,128)(2,1)} %bitcast.9), custom_call_target="tpu_custom_call" | custom-call | tf_op jit(solution)/shard_map/pallas_call | solution.py:806
  86.4 0.5 slice.3
  87.6 0.0 copy-done
  87.6 0.0 copy-done.1
  87.6 0.0 copy-done.2
  87.6 0.0 copy-done.3
  87.7 120.1 %conditional.1 = (bf16[1024,640]{1,0:T(8,128)(2,1)}, bf16[4096,640]{1,0:T(8,128)(2,1)}, f32[]{:T(128)}) conditional(s32[]{:T(128)} %bitcast.8, (s32[8,128]{1,0:T(8,128)S(1)}, bf16[16,128,640]{2,1,0:T(8,128)(2,1)}, bf16[1024,640]{1,0:T(8,128)(2,1)S(1)}, f32[8,128]{1,0:T(8,128)S(1)}) %tuple.20, (s32[1024]{0:T(1024)S(1)}, ...), branch_computations={%region_0.0_spmd, %region_1.0_spmd} | conditional | bytes 24 | solution.py:878
  87.7 113.5 %branch_1_fun.2 = (bf16[1024,640]{1,0:T(8,128)(2,1)}, bf16[16,128,640]{2,1,0:T(8,128)(2,1)}, f32[8,128]{1,0:T(8,128)}, s32[8,128]{1,0:T(8,128)}) custom-call(s32[8,8]{1,0:T(8,128)S(1)} %get-tuple-element.31.lists, s32[8,128]{1,0:T(8,128)S(1)} %bitcast.12, bf16[1024,640]{1,0:T(8,128)(2,1)S(1)} %get-tuple-element.33.emb_hbm, bf16[32,128,640]{2,1,0:T(8,128)(2,1)S(1)} %bitcast.10), custom_call_target="tpu_custom_call" | custom-call | tf_op jit(solution)/shard_map/cond/branch_1_fun/pallas_call | solution.py:806
  201.2 6.6 %branch_1_fun.3 = (bf16[32,128,640]{2,1,0:T(8,128)(2,1)}, bf16[1024,640]{1,0:T(8,128)(2,1)}, f32[1,1]{1,0:T(1,128)}) custom-call(s32[8,128]{1,0:T(8,128)} %get-tuple-element.35.plan, bf16[16,128,640]{2,1,0:T(8,128)(2,1)} %get-tuple-element.36.returned, bf16[1024,640]{1,0:T(8,128)(2,1)} %get-tuple-element.37.emb_in, f32[8,128]{1,0:T(8,128)} %get-tuple-element.38.loss_in), custom_call_target="tpu_custom_call" | custom-call | tf_op jit(solution)/shard_map/cond/branch_1_fun/pallas_call | solution.py:221
Async XLA Ops:
  0.6 87.0 %copy-start = (bf16[4096,640]{1,0:T(8,128)(2,1)S(1)}, bf16[4096,640]{1,0:T(8,128)(2,1)}, u32[]{:S(2)}) copy-start(bf16[4096,640]{1,0:T(8,128)(2,1)} %param.7) | copy-start | bytes 15728644
  0.6 87.0 %copy-start.1 = (bf16[1024,640]{1,0:T(8,128)(2,1)S(1)}, bf16[1024,640]{1,0:T(8,128)(2,1)}, u32[]{:S(2)}) copy-start(bf16[1024,640]{1,0:T(8,128)(2,1)} %emb_hbm.1) | copy-start | bytes 3932164
  0.7 87.0 %copy-start.2 = (s32[8,8]{1,0:T(8,128)S(1)}, s32[8,8]{1,0:T(8,128)}, u32[]{:S(2)}) copy-start(s32[8,8]{1,0:T(8,128)} %lists.1) | copy-start | bytes 772
  0.7 87.0 %copy-start.3 = (s32[1024]{0:T(1024)S(1)}, s32[1024]{0:T(1024)}, u32[]{:S(2)}) copy-start(s32[1024]{0:T(1024)} %param.9) | copy-start | bytes 12292

commit v4 on v3

--- a/solution.py
+++ b/solution.py
@@ -14,8 +14,12 @@
 PARTS = 8
 CHUNK = {False: 64, True: 256}
 DZ_CHUNK = 256
+LAG_FIRST = 4
 LAG = 4
+LAG_LAST = 4
+DZ_FIRST = 1
 DZ_LAG = 4
+DZ_LAST = 1
 CODE_MAX = 32766.0
 GUARD = 1
 BOUND = 48.0
@@ -564,9 +568,15 @@
             bound_copy(way, g).start()
             bound_top[...] = jnp.maximum(bound_top[...], bound_out[way, g])
 
-    dz_start = (parts - 1) * chunks + LAG * last
+    def lag(hops, first, middle, final):
+        between = jnp.maximum(jnp.minimum(hops - 1, last - 2), 0) * middle
+        return jnp.where(hops == 0, 0, first + between + jnp.where(hops == last, final, 0))
+
+    part_total = LAG_FIRST + max(last - 2, 0) * LAG + LAG_LAST
+    dz_total = DZ_FIRST + max(last - 2, 0) * DZ_LAG + DZ_LAST
+    dz_start = (parts - 1) * chunks + part_total
     tail_start = ratio * dz_chunks
-    ret_start = -(-(dz_start + tail_start + DZ_LAG * last) // dz_chunks) * dz_chunks
+    ret_start = -(-(dz_start + tail_start + dz_total) // dz_chunks) * dz_chunks
 
     def send_pieces(q):
         out = lax.dot_general(
@@ -639,7 +649,22 @@
                 def _():
                     tiles_in(g)
 
-            new_block(at // chunks)
+            g = at // chunks
+            new_block(g)
+
+            @pl.when((z == 0) | (z == last))
+            def _():
+                way = jnp.where(z == 0, 0, 1)
+                if coded:
+                    new_bound(way, g, jnp.int32(0))
+
+                def first_hop(c, carry):
+                    if coded:
+                        encode(way, g, c, scores[g, pl.ds(rows_of(way, c * chunk), chunk), :])
+                    part_copy(way, g, c, True).start()
+                    return carry
+
+                lax.fori_loop(0, chunks, first_hop, 0)
 
         @pl.when(at == ret_start)
         def _():
@@ -653,9 +678,9 @@
         way = lax.rem(i, 2)
         s = at + i // 2
         pos = jnp.where(way == 0, z, last - z)
-        turn = s - LAG * pos
-
-        @pl.when((turn >= 0) & (turn < parts * chunks))
+        turn = s - lag(pos, LAG_FIRST, LAG, LAG_LAST)
+
+        @pl.when((turn >= 0) & (turn < parts * chunks) & (pos > 0))
         def _():
             g = turn // chunks
             c = lax.rem(turn, chunks)
@@ -668,13 +693,7 @@
 
             at = pl.ds(rows_of(way, c * chunk), chunk)
 
-            @pl.when(pos == 0)
-            def _():
-                if coded:
-                    encode(way, g, c, scores[g, at, :])
-                part_copy(way, g, c, True).start()
-
-            @pl.when((pos > 0) & (pos < last))
+            @pl.when(pos < last)
             def _():
                 part_copy(way, g, c, False).wait_recv()
                 value = decode(way, g, c) + scores[g, at, :]
@@ -693,7 +712,7 @@
             def _():
                 lax.fori_loop(0, chunk // SOFT, softmax_rows, rows_of(way, c * chunk))
 
-        d = s - dz_start - DZ_LAG * (last - pos)
+        d = s - dz_start - lag(last - pos, DZ_FIRST, DZ_LAG, DZ_LAST)
         u = jnp.where(d < tail_start, d // ratio, d - tail_start + dz_chunks)
         now = (d >= 0) & (u < parts * dz_chunks)
         now = now & ((d >= tail_start) | (lax.rem(d + ratio, ratio) == ratio - 1))
@@ -702,9 +721,17 @@
         def _():
             dz_copy(way, u).wait_recv()
 
-        @pl.when(now & (pos > 0))
+        @pl.when(now & (pos > 0) & ((pos < last) | (u < dz_chunks)))
         def _():
             dz_copy(way, u).start()
+
+        @pl.when(now & (pos == last) & (u == dz_chunks - 1))
+        def _():
+            def rest(later, carry):
+                dz_copy(way, later).start()
+                return carry
+
+            lax.fori_loop(dz_chunks, parts * dz_chunks, rest, 0)
 
         return at
 

time: 210 us -> 207 us (0.986); the launches traced: 208 us -> 207 us
  no operation moved by 1% of the time
where the time goes in v4:
time: 207 us
  Pallas kernels  205 us (99%)
    pallas_call x2, Pallas kernels, run_main(): pl.pallas_call(functools.partial(main_kernel, coded, groups, dp_count, ti...  199 us
    pallas_call x1, Pallas kernels, place_tiles(): pl.pallas_call(place_kernel, out_shape=(jax.ShapeDtypeStruct((tiles_here,...  6.6 us

profile of v4, /device:TPU:0, one launch (start us, length us, event | category | flops | bytes accessed | tf_op | source)
XLA Modules:
  0.0 207.1 jit_solution(2921804962673826539)
XLA Ops:
  0.6 0.0 copy-start
  0.6 0.0 copy-start.1
  0.7 0.0 copy-start.2
  0.7 0.0 copy-start.3
  0.7 84.9 %shard_map.67 = (bf16[1024,640]{1,0:T(8,128)(2,1)S(1)}, bf16[16,128,640]{2,1,0:T(8,128)(2,1)}, f32[8,128]{1,0:T(8,128)S(1)}, s32[8,128]{1,0:T(8,128)S(1)}) custom-call(s32[8,8]{1,0:T(8,128)} %lists.1, s32[8,128]{1,0:T(8,128)} %bitcast.11, bf16[1024,640]{1,0:T(8,128)(2,1)} %emb_hbm.1, bf16[32,128,640]{2,1,0:T(8,128)(2,1)} %bitcast.9), custom_call_target="tpu_custom_call" | custom-call | tf_op jit(solution)/shard_map/pallas_call | solution.py:833
  85.5 0.5 slice.3
  86.7 0.0 copy-done
  86.7 0.0 copy-done.1
  86.7 0.0 copy-done.2
  86.7 0.0 copy-done.3
  86.7 120.3 %conditional.1 = (bf16[1024,640]{1,0:T(8,128)(2,1)}, bf16[4096,640]{1,0:T(8,128)(2,1)}, f32[]{:T(128)}) conditional(s32[]{:T(128)} %bitcast.8, (s32[8,128]{1,0:T(8,128)S(1)}, bf16[16,128,640]{2,1,0:T(8,128)(2,1)}, bf16[1024,640]{1,0:T(8,128)(2,1)S(1)}, f32[8,128]{1,0:T(8,128)S(1)}) %tuple.20, (s32[1024]{0:T(1024)S(1)}, ...), branch_computations={%region_0.0_spmd, %region_1.0_spmd} | conditional | bytes 24 | solution.py:905
  86.8 113.7 %branch_1_fun.2 = (bf16[1024,640]{1,0:T(8,128)(2,1)}, bf16[16,128,640]{2,1,0:T(8,128)(2,1)}, f32[8,128]{1,0:T(8,128)}, s32[8,128]{1,0:T(8,128)}) custom-call(s32[8,8]{1,0:T(8,128)S(1)} %get-tuple-element.31.lists, s32[8,128]{1,0:T(8,128)S(1)} %bitcast.12, bf16[1024,640]{1,0:T(8,128)(2,1)S(1)} %get-tuple-element.33.emb_hbm, bf16[32,128,640]{2,1,0:T(8,128)(2,1)S(1)} %bitcast.10), custom_call_target="tpu_custom_call" | custom-call | tf_op jit(solution)/shard_map/cond/branch_1_fun/pallas_call | solution.py:833
  200.5 6.6 %branch_1_fun.3 = (bf16[32,128,640]{2,1,0:T(8,128)(2,1)}, bf16[1024,640]{1,0:T(8,128)(2,1)}, f32[1,1]{1,0:T(1,128)}) custom-call(s32[8,128]{1,0:T(8,128)} %get-tuple-element.35.plan, bf16[16,128,640]{2,1,0:T(8,128)(2,1)} %get-tuple-element.36.returned, bf16[1024,640]{1,0:T(8,128)(2,1)} %get-tuple-element.37.emb_in, f32[8,128]{1,0:T(8,128)} %get-tuple-element.38.loss_in), custom_call_target="tpu_custom_call" | custom-call | tf_op jit(solution)/shard_map/cond/branch_1_fun/pallas_call | solution.py:225
Async XLA Ops:
  0.6 86.1 %copy-start = (bf16[4096,640]{1,0:T(8,128)(2,1)S(1)}, bf16[4096,640]{1,0:T(8,128)(2,1)}, u32[]{:S(2)}) copy-start(bf16[4096,640]{1,0:T(8,128)(2,1)} %param.7) | copy-start | bytes 15728644
  0.6 86.1 %copy-start.1 = (bf16[1024,640]{1,0:T(8,128)(2,1)S(1)}, bf16[1024,640]{1,0:T(8,128)(2,1)}, u32[]{:S(2)}) copy-start(bf16[1024,640]{1,0:T(8,128)(2,1)} %emb_hbm.1) | copy-start | bytes 3932164
  0.7 86.1 %copy-start.2 = (s32[8,8]{1,0:T(8,128)S(1)}, s32[8,8]{1,0:T(8,128)}, u32[]{:S(2)}) copy-start(s32[8,8]{1,0:T(8,128)} %lists.1) | copy-start | bytes 772
  0.7 86.1 %copy-start.3 = (s32[1024]{0:T(1024)S(1)}, s32[1024]{0:T(1024)}, u32[]{:S(2)}) copy-start(s32[1024]{0:T(1024)} %param.9) | copy-start | bytes 12292
